TPU v7x, 32 devices: a whole 2x2x4 slice. The times are simulated.
32 devices in a mesh: win: 8 (over z, x), frm: 4 (over y, core).
Axes of the slice: x: 2, y: 2, z: 4, core: 2. Of those that a mesh axis runs over, the one named last changes fastest.
Arguments:
- tokens: bfloat16 [64, 512, 1024], P('win', 'frm'), may hold values from -6 to 6
- condition: bfloat16 [64, 1024], P('win'), may hold values from -6 to 6
- doubled: int32 [64], P('win'), may hold values from 0 to 3
- window_count: int32 [8], P('win'), may hold values from 4 to 8, as said below
- w_ada: bfloat16 [1024, 6144], P('win'), may hold values from -0.1875 to 0.1875
- b_ada: bfloat16 [6144], P('win'), may hold values from -3 to 3
- w_qkv: bfloat16 [1024, 3072], P('win'), may hold values from -0.1875 to 0.1875
- w_out: bfloat16 [1024, 1024], P('win'), may hold values from -1.5 to 1.5
- w_up: bfloat16 [1024, 4096], P('win'), may hold values from -0.1875 to 0.1875
- b_up: bfloat16 [4096], P('win'), may hold values from -3 to 3
- w_down: bfloat16 [4096, 1024], P('win'), may hold values from -0.09375 to 0.09375
- b_down: bfloat16 [1024], P('win'), may hold values from -3 to 3
- table_space: float32 [16, 225], replicated, may hold values from -4 to 4
- table_time: float32 [16, 9], replicated, may hold values from -4 to 4
- cotangent: bfloat16 [64, 512, 1024], P('win', 'frm'), may hold values from -6 to 6
Outputs:
- output: bfloat16 [64, 512, 1024], P('win', 'frm')
- grad_tokens: float32 [64, 512, 1024], P('win', 'frm')
- grad_condition: float32 [64, 1024], P('win')
- grad_w_ada: float32 [1024, 6144], P(None, ('win', 'frm'))
- grad_b_ada: float32 [6144], P(('win', 'frm'))
- grad_w_qkv: float32 [1024, 3072], P(None, ('win', 'frm'))
- grad_w_out: float32 [1024, 1024], P(None, ('win', 'frm'))
- grad_w_up: float32 [1024, 4096], P(None, ('win', 'frm'))
- grad_b_up: float32 [4096], P(('win', 'frm'))
- grad_w_down: float32 [4096, 1024], P(('win', 'frm'))
- grad_b_down: float32 [1024], P(('win', 'frm'))
- grad_table_space: float32 [16, 225], replicated
- grad_table_time: float32 [16, 9], replicated
Inputs may be any that keep to these rules, and one draw needn't show every extreme that they name: `window_count`: each index of win has at most 8 live windows, its first ones; some index has exactly 8.
All inputs are finite; a program needn't handle non-finite values.
Results may differ from a plain program's by a relative error of at most 0.018.
Values may be sent and summed in bfloat16 or wider, within the bound.
No kernel may reach another device: no remote copies, remote signals or barrier semaphores. Data moves between devices by JAX's collectives and lax.ppermute only.
A program may use at most 320 MiB of HBM per device.

v0:
```python
import functools

import jax
import jax.numpy as jnp
from jax import lax
from jax.experimental import pallas as pl
from jax.experimental.pallas import tpu as pltpu
from jax.sharding import PartitionSpec as P

SIDE = 8
FRAMES = 5
SPATIAL = SIDE * SIDE
BOTH = ("win", "frm")
EPS = 1e-06
VMEM_LIMIT = 50 * 1024 * 1024
WHOLE_LIMIT = 60 * 1024 * 1024

f32 = jnp.float32
bf16 = jnp.bfloat16
exact_mode = lax.Precision.HIGHEST
SMALL = pl.CostEstimate(flops=1024, bytes_accessed=1024, transcendentals=0)


def swap_frm(array, bit):
    return lax.ppermute(array, "frm", [(j, j ^ bit) for j in range(4)])


def swap_core(array):
    return swap_frm(array, 1)


def swap_y(array):
    return swap_frm(array, 2)


def swap_win(array, bits):
    count = lax.axis_size("win")
    return lax.ppermute(array, "win", [(j, j ^ bits) for j in range(count)])


def exchange_all(array):
    return lax.all_to_all(array, BOTH, split_axis=0, concat_axis=0, tiled=True)


def pick(array, index, axis):
    return lax.dynamic_index_in_dim(array, index, axis, keepdims=False)


def sync(*arrays):
    return lax.optimization_barrier(arrays)


def exchange_z(blocks):
    groups = [[2 * z + x for z in range(4)] for x in range(2)]
    return lax.all_to_all(
        blocks, "win", split_axis=0, concat_axis=0, axis_index_groups=groups, tiled=True
    )


def gather_z(half):
    return exchange_z(jnp.broadcast_to(half[None], (4,) + half.shape))


def gather_z_direct(half):
    return [half] + [swap_win(half, 2 * k) for k in (1, 2, 3)]


def move_kernel(body, count, where, *refs):
    sems = refs[count]
    refs = refs[:count] + refs[count + 1 :]
    waits = []

    def copy(sources, target):
        sem = sems.at[len(waits)]
        if len(sources) == 1:
            pltpu.make_async_copy(sources[0], target, sem).start()
        else:
            condition, first, second = sources

            @pl.when(condition)
            def _():
                pltpu.make_async_copy(first, target, sem).start()

            @pl.when(jnp.logical_not(condition))
            def _():
                pltpu.make_async_copy(second, target, sem).start()

        waits.append(pltpu.make_async_copy(sources[-1], target, sem))

    def finish():
        for wait in waits:
            wait.wait()

    body(where, refs, copy, finish)


def move_call(body, name, where, inputs, outputs, copies, scratch=(), limit=VMEM_LIMIT):
    return pl.pallas_call(
        functools.partial(move_kernel, body, len(inputs) + len(outputs)),
        out_shape=outputs,
        in_specs=[pl.BlockSpec(memory_space=pltpu.SMEM)]
        + [pl.BlockSpec(memory_space=pltpu.HBM)] * len(inputs),
        out_specs=[pl.BlockSpec(memory_space=pltpu.VMEM)] * len(outputs),
        scratch_shapes=[pltpu.SemaphoreType.DMA((copies,))] + list(scratch),
        compiler_params=pltpu.CompilerParams(vmem_limit_bytes=limit),
        cost_estimate=SMALL,
        name=name,
    )(where, *inputs)


def low_shape(*shape):
    return jax.ShapeDtypeStruct(shape, bf16)


def halves(where, w_qkv, w_out, w_up, w_down):
    rows, width = w_out.shape
    blocks = w_up.shape[1] // 256
    block = w_down.shape[0] // 4

    def body(where, refs, copy, finish):
        qkv, out, up, down, q_half, up_half, down_half = refs
        y, c = where[2], where[3]
        quarter = rows // 4
        q_rows = pl.ds(pl.multiple_of((c * 2 + y) * quarter, quarter), quarter)
        copy([qkv.at[q_rows]], q_half.at[:, pl.ds(0, 3 * width)])
        copy([out.at[q_rows]], q_half.at[:, pl.ds(3 * width, width)])
        up_rows = pl.ds(pl.multiple_of(y * (rows // 2), rows // 2), rows // 2)
        for n in range(blocks):
            column = pl.multiple_of((2 * n + c) * 128, 128)
            copy([up.at[up_rows, pl.ds(column, 128)]], up_half.at[:, pl.ds(n * 128, 128)])
        copy([down.at[pl.ds(pl.multiple_of((y * 2 + c) * block, block), block)]], down_half)
        finish()

    return move_call(
        body,
        "halves",
        where,
        [w_qkv, w_out, w_up, w_down],
        [
            low_shape(rows // 4, 4 * width),
            low_shape(rows // 2, blocks * 128),
            low_shape(block, width),
        ],
        blocks + 3,
        limit=WHOLE_LIMIT,
    )


def gather_near(along_z):
    return [along_z, swap_win(along_z, 1), swap_y(along_z)]


def gather_far(near, cut=0):
    if not cut:
        return [swap_win(near[2], 1)]
    return [swap_y(near[1][:cut]), swap_win(near[2][cut:], 1)]


PLACES = ((0, 0), (1, 0), (0, 1), (1, 1))


def piece(refs, number, k):
    if number < 3 or len(refs) == 4:
        return refs[number].at[k]
    cut = refs[3].shape[0]
    return refs[3].at[k] if k < cut else refs[4].at[k - cut]


def place_qkv(where, pieces):
    _, rows, columns = pieces[0].shape
    width = columns // 4

    def body(where, refs, copy, finish):
        z, x, y, c = where[0], where[1], where[2], where[3]
        for core in range(2):
            for n, (j, l) in enumerate(PLACES):
                for k in range(4):
                    source = piece(refs[4 * core : 4 * core + 4], n, k)
                    at = ((z ^ k) * 2 + (x ^ j), c ^ core, y ^ l)
                    copy([source.at[:, pl.ds(0, 3 * width)]], refs[8].at[at])
                    copy([source.at[:, pl.ds(3 * width, width)]], refs[9].at[at])
        finish()

    qkv, out = move_call(
        body,
        "place_qkv",
        where,
        pieces,
        [low_shape(8, 2, 2, rows, 3 * width), low_shape(8, 2, 2, rows, width)],
        64,
    )
    return qkv.reshape(32 * rows, 3 * width), out.reshape(32 * rows, width)


def place_up(where, pieces):
    _, rows, columns = pieces[0].shape

    def body(where, refs, copy, finish):
        z, x, y = where[0], where[1], where[2]
        for n, (j, l) in enumerate(PLACES):
            for k in range(4):
                copy([piece(refs[:4], n, k)], refs[4].at[(z ^ k) * 2 + (x ^ j), y ^ l])
        finish()

    return move_call(
        body, "place_up", where, pieces, [low_shape(8, 2, rows, columns)], 16
    )[0].reshape(16 * rows, columns)


def place_down(where, pieces):
    _, rows, columns = pieces[0].shape

    def body(where, refs, copy, finish):
        for n in range(4):
            for k in range(4):
                quarter = QUARTERS.index(PLACES[n])
                copy([piece(refs[:5], n, k)], refs[5].at[quarter, where[0] ^ k])
        finish()

    return move_call(
        body, "place_down", where, pieces, [low_shape(4, 4, rows, columns)], 16
    )[0].reshape(16 * rows, columns)


QUARTERS = ((1, 1), (1, 0), (0, 1), (0, 0))


FAR_CUT = 2
LAST_CUT = 1


def add_low(*terms):
    return functools.reduce(jnp.add, [term.astype(f32) for term in terms]).astype(bf16)


def block_specs(array, first, cut=0):
    if array.ndim == 4:
        return pl.BlockSpec((1, 1) + array.shape[2:], lambda i: (first, i, 0, 0))
    rows = array.shape[0] // (4 if first is None else first)
    last = array.shape[0] // rows - 1
    return pl.BlockSpec((rows, array.shape[1]), lambda i: (jnp.clip(i - cut, 0, last), 0))


def read(ref):
    return ref[...].reshape(ref.shape[-2:]).astype(f32)


def merge_kernel(counts, cut, *refs):
    x_terms, y_terms = refs[: counts[0]], refs[counts[0] : counts[0] + counts[1]]
    far_y, far_x, send_x, send_y = refs[-4:]
    first = pl.program_id(0) < cut
    to_x = functools.reduce(jnp.add, [read(ref) for ref in x_terms])
    to_y = functools.reduce(jnp.add, [read(ref) for ref in y_terms])
    send_x[...] = jnp.where(first, to_x + read(far_y), to_x).astype(bf16)
    send_y[...] = jnp.where(first, to_y, to_y + read(far_x)).astype(bf16)


def merge(x_terms, y_terms, far_y, far_x, cut=FAR_CUT):
    rows, width = far_y.shape[0] // cut, far_y.shape[1]
    block = pl.BlockSpec((rows, width), lambda i: (i, 0))
    return dense_call(
        functools.partial(merge_kernel, (len(x_terms), len(y_terms)), cut),
        "merge",
        (4,),
        [block_specs(*term) for term in list(x_terms) + list(y_terms)]
        + [block_specs(far_y, cut), block_specs(far_x, 4 - cut, cut)],
        [block, block],
        [low_shape(4 * rows, width)] * 2,
    )(*[term[0] for term in list(x_terms) + list(y_terms)], far_y, far_x)


def total_kernel(*refs):
    refs[-1][...] = functools.reduce(jnp.add, [read(ref) for ref in refs[:-1]]).astype(bf16)


def total(terms, rows, width):
    return dense_call(
        total_kernel,
        "total",
        (4,),
        [block_specs(*term) for term in terms],
        pl.BlockSpec((rows, width), lambda i: (i, 0)),
        low_shape(4 * rows, width),
    )(*[term[0] for term in terms])


def first_kernel(own_ref, got_ref, far_y, far_x, x_ref):
    far = own_ref[0].astype(f32) + got_ref[0].astype(f32)
    far_y[...] = far[:LAST_CUT].astype(bf16).reshape(far_y.shape)
    far_x[...] = far[LAST_CUT:].astype(bf16).reshape(far_x.shape)
    x_ref[...] = (own_ref[1].astype(f32) + got_ref[1].astype(f32)).astype(bf16).reshape(x_ref.shape)


def first_quarters(own, got):
    _, _, rows, width = own.shape
    shapes = [(LAST_CUT * rows, width), ((4 - LAST_CUT) * rows, width), (4 * rows, width)]
    return dense_call(
        first_kernel,
        "first_quarters",
        (1,),
        [full_spec(own.shape)] * 2,
        [full_spec(shape) for shape in shapes],
        [low_shape(*shape) for shape in shapes],
    )(own, got)


def parts_z(kept):
    return exchange_z(kept.reshape((4, kept.shape[0] // 4) + kept.shape[1:]))


def add_z(parts):
    return jnp.sum(parts.astype(f32), axis=0)


def sum_z_direct(kept, z):
    blocks = kept.reshape((4, kept.shape[0] // 4) + kept.shape[1:])
    sent = [swap_win(pick(blocks, z ^ k, 0), 2 * k) for k in (1, 2, 3)]
    return functools.reduce(jnp.add, [part.astype(f32) for part in [pick(blocks, z, 0)] + sent])


def scatter_plain(grad, where):
    mine = lax.psum_scatter(grad.astype(f32), "win", scatter_dimension=0, tiled=False)
    return pick(mine, where[2], 0) + swap_y(pick(mine, 1 - where[2], 0))


def windows_send(where, slots):
    def body(where, refs, copy, finish):
        for half in range(2):
            first = half * 8 + (1 - where[3]) * 4
            copy([refs[0].at[pl.ds(first, 4)]], refs[1].at[pl.ds(half * 4, 4)])
        finish()

    return move_call(body, "rows_send", where, [slots], [low_shape(8, *slots.shape[1:])], 2, limit=WHOLE_LIMIT)[0]


def windows_pack(where, slots, got):
    def body(where, refs, copy, finish):
        own, other, here, away = refs
        y, c = where[2], where[3]
        for target, half in ((here, y), (away, 1 - y)):
            for t in range(2):
                window = half * 4 + c * 2 + t
                mine, theirs = window * 2, half * 4 + t * 2
                copy([c == 0, own.at[mine], other.at[theirs]], target.at[t * 3])
                copy([c == 0, other.at[theirs], own.at[mine]], target.at[t * 3 + 1])
                copy(
                    [where[6 + window] == where[4], own.at[mine + 1], other.at[theirs + 1]],
                    target.at[t * 3 + 2],
                )
        finish()

    shape = low_shape(6, *slots.shape[1:])
    return move_call(body, "rows_pack", where, [slots, got], [shape, shape], 12)


def windows_join(where, here, away):
    def body(where, refs, copy, finish):
        here, away, out = refs
        y = where[2]
        for t in range(2):
            for slot in range(4):
                source = t * 3 + slot % 2
                copy([y == slot // 2, here.at[source], away.at[source]], out.at[t * 5 + slot])
            near = where[6 + where[4] * 2 + t] // 2 == y
            copy([near, here.at[t * 3 + 2], away.at[t * 3 + 2]], out.at[t * 5 + 4])
        finish()

    shape = low_shape(10, *here.shape[1:])
    out = move_call(body, "rows_join", where, [here, away], [shape], 10)[0]
    return out.reshape(10 * here.shape[1], here.shape[2])


def windows_back_pack(where, rows, back):
    def body(where, refs, copy, finish):
        rows, back, out = refs
        y, c = where[2], where[3]
        for t in range(2):
            here, there = y * 4 + t * 2, (1 - y) * 4 + t * 2
            copy([rows.at[t * 5 + 2 * y + 1 - c]], out.at[here])
            copy([rows.at[t * 5 + 4]], out.at[here + 1])
            copy([back.at[t * 3 + 1 - c]], out.at[there])
            copy([back.at[t * 3 + 2]], out.at[there + 1])
        finish()

    slots = rows.reshape(10, SPATIAL, rows.shape[1])
    shape = low_shape(8, SPATIAL, rows.shape[1])
    return move_call(body, "rows_back_pack", where, [slots, back], [shape], 8)[0]


def windows_back_join(where, rows, back, got, dead, dtype):
    width = rows.shape[1]

    def body(where, refs, copy, finish):
        rows, back, got, dead, out, arrived = refs
        y, c, frm, count = where[2], where[3], where[4], where[5]
        for half in range(2):
            side = y if half == 0 else 1 - y
            for core in range(2):
                for t in range(2):
                    window = side * 4 + (c if core == 0 else 1 - c) * 2 + t
                    if core == 1:
                        even, odd = got.at[side * 4 + t * 2], got.at[side * 4 + t * 2 + 1]
                    elif half == 0:
                        even, odd = rows.at[t * 5 + 2 * y + c], rows.at[t * 5 + 4]
                    else:
                        even, odd = back.at[t * 3 + c], back.at[t * 3 + 2]
                    live = window < count
                    place = window * 2
                    copy([live, even, dead.at[place]], arrived.at[place])
                    doubled = jnp.logical_and(live, where[6 + window] == frm)
                    copy([doubled, odd, dead.at[place + 1]], arrived.at[place + 1])
        finish()
        out[...] = arrived[...].astype(out.dtype)

    slots = rows.reshape(10, SPATIAL, width)
    out = move_call(
        body,
        "rows_back_join",
        where,
        [slots, back, got, dead.reshape(16, SPATIAL, width)],
        [jax.ShapeDtypeStruct((16, SPATIAL, width), dtype)],
        16,
        [pltpu.VMEM((16, SPATIAL, width), bf16)],
    )[0]
    return out.reshape(dead.shape)


GROUP = 4
LANES = GROUP * 64


def head_lanes(head):
    lanes = lax.broadcasted_iota(jnp.int32, (1, LANES), 1)
    return (lanes // 64) == head


def attend_kernel(q_ref, k_ref, v_ref, space_ref, time_ref, o_ref, p_ref):
    q, k, v = q_ref[...], k_ref[...], v_ref[...]
    rows = q.shape[0]
    total = jnp.zeros((rows, LANES), f32)
    for head in range(GROUP):
        lanes = head_lanes(head)
        scaled = jnp.where(lanes, q * jnp.asarray(0.125, bf16), jnp.zeros_like(q))
        scores = lax.dot_general(scaled, k, (((1,), (1,)), ((), ())), preferred_element_type=f32)
        shaped = scores.reshape(rows // SPATIAL, SPATIAL, rows)
        shaped = shaped + space_ref[head][None] + time_ref[0, head, : rows // SPATIAL][:, None, :]
        scores = shaped.reshape(rows, rows)
        grown = jnp.exp(scores - jnp.max(scores, axis=-1, keepdims=True))
        inverse = 1.0 / jnp.sum(grown, axis=-1, keepdims=True)
        probs = (grown * inverse).astype(bf16)
        p_ref[0, head] = probs
        masked = jnp.where(lanes, v, jnp.zeros_like(v))
        total = total + jnp.dot(probs, masked, preferred_element_type=f32)
    o_ref[...] = total.astype(bf16)


def attend_back_kernel(
    q_ref, k_ref, v_ref, do_ref, o_ref, p_ref, grad_ref, space_ref, time_ref
):
    q, k, v, do = q_ref[...], k_ref[...], v_ref[...], do_ref[...]
    rows = q.shape[0]
    slots = rows // SPATIAL
    product = do.astype(f32) * o_ref[...].astype(f32)
    grad_q = jnp.zeros((rows, LANES), f32)
    grad_k = jnp.zeros((rows, LANES), f32)
    grad_v = jnp.zeros((rows, LANES), f32)

    @pl.when(pl.program_id(1) == 0)
    def _():
        space_ref[...] = jnp.zeros_like(space_ref)

    for head in range(GROUP):
        lanes = head_lanes(head)
        none = jnp.zeros_like(q)
        scale = jnp.asarray(0.125, bf16)
        row_dot = jnp.sum(jnp.where(lanes, product, 0.0), axis=-1, keepdims=True)
        grads = jnp.where(lanes, do, none)
        probs = p_ref[0, head]
        grad_probs = lax.dot_general(
            grads, v, (((1,), (1,)), ((), ())), preferred_element_type=f32
        )
        grad_scores = probs.astype(f32) * (grad_probs - row_dot)
        low = grad_scores.astype(bf16)
        over_rows = (((0,), (0,)), ((), ()))
        grad_v = grad_v + lax.dot_general(probs, grads, over_rows, preferred_element_type=f32)
        grad_k = grad_k + lax.dot_general(
            low, jnp.where(lanes, q * scale, none), over_rows, preferred_element_type=f32
        )
        grad_q = grad_q + jnp.dot(
            low, jnp.where(lanes, k * scale, none), preferred_element_type=f32
        )
        shaped = grad_scores.reshape(slots, SPATIAL, rows)
        space_ref[head] += jnp.sum(shaped, axis=0)
        time_ref[0, head, :slots] = jnp.sum(shaped, axis=1)
    grad_ref[0] = grad_q.astype(bf16)
    grad_ref[1] = grad_k.astype(bf16)
    grad_ref[2] = grad_v.astype(bf16)


def attention_specs(rows, groups):
    q_spec = pl.BlockSpec((rows, LANES), lambda group, window: (window, group))
    k_spec = pl.BlockSpec((rows, LANES), lambda group, window: (window, group + groups))
    v_spec = pl.BlockSpec((rows, LANES), lambda group, window: (window, group + 2 * groups))
    p_spec = pl.BlockSpec((1, GROUP, rows, rows), lambda group, window: (window, group, 0, 0))
    space_spec = pl.BlockSpec((GROUP, SPATIAL, rows), lambda group, window: (group, 0, 0))
    time_spec = pl.BlockSpec((1, GROUP, 8, rows), lambda group, window: (window, group, 0, 0))
    return q_spec, k_spec, v_spec, p_spec, space_spec, time_spec


def attend(projected, space_bias, time_bias, windows):
    rows = projected.shape[0] // windows
    heads = space_bias.shape[0]
    q_spec, k_spec, v_spec, p_spec, space_spec, time_spec = attention_specs(rows, heads // GROUP)
    width = heads * 64
    return pl.pallas_call(
        attend_kernel,
        grid=(heads // GROUP, windows),
        in_specs=[q_spec, k_spec, v_spec, space_spec, time_spec],
        out_specs=[q_spec, p_spec],
        out_shape=[
            pltpu.HBM((windows * rows, width), bf16),
            pltpu.HBM((windows, heads, rows, rows), bf16),
        ],
        compiler_params=pltpu.CompilerParams(vmem_limit_bytes=VMEM_LIMIT),
        cost_estimate=SMALL,
        name="attend",
    )(projected, projected, projected, space_bias, time_bias)


def attend_back(projected, grad_attended, attended, probs, windows):
    heads, rows = probs.shape[1], probs.shape[2]
    q_spec, k_spec, v_spec, p_spec, space_spec, time_spec = attention_specs(rows, heads // GROUP)
    width = heads * 64
    return pl.pallas_call(
        attend_back_kernel,
        grid=(heads // GROUP, windows),
        in_specs=[q_spec, k_spec, v_spec, q_spec, q_spec, p_spec],
        out_specs=[
            pl.BlockSpec((3, rows, LANES), lambda group, window: (0, window, group)),
            space_spec,
            time_spec,
        ],
        out_shape=[
            pltpu.HBM((3, windows * rows, width), bf16),
            pltpu.HBM((heads, SPATIAL, rows), f32),
            pltpu.HBM((windows, heads, 8, rows), f32),
        ],
        compiler_params=pltpu.CompilerParams(vmem_limit_bytes=VMEM_LIMIT),
        cost_estimate=SMALL,
        name="attend_back",
    )(projected, projected, projected, grad_attended, attended, probs)


def full_spec(shape):
    return pl.BlockSpec(shape, lambda *_: (0,) * len(shape))


def in_hbm(shapes):
    if isinstance(shapes, list):
        return [in_hbm(shape) for shape in shapes]
    return pltpu.HBM(shapes.shape, shapes.dtype)


def dense_call(kernel, name, grid, in_specs, out_specs, out_shape, scratch=()):
    return pl.pallas_call(
        kernel,
        grid=grid,
        in_specs=in_specs,
        out_specs=out_specs,
        out_shape=in_hbm(out_shape),
        scratch_shapes=list(scratch),
        compiler_params=pltpu.CompilerParams(vmem_limit_bytes=VMEM_LIMIT),
        cost_estimate=SMALL,
        name=name,
    )


def normalize(values_in):
    centred = values_in - jnp.mean(values_in, axis=-1, keepdims=True)
    inverse = lax.rsqrt(jnp.mean(centred * centred, axis=-1, keepdims=True) + EPS)
    return centred * inverse, inverse


def normalize_back(grad_normed, normed, inverse):
    return inverse * (
        grad_normed
        - jnp.mean(grad_normed, axis=-1, keepdims=True)
        - normed * jnp.mean(grad_normed * normed, axis=-1, keepdims=True)
    )


def dot32(left, right, dims):
    return lax.dot_general(left, right, (dims, ((), ())), preferred_element_type=f32)


def modulation(mod_ref, number, window=0):
    width = mod_ref.shape[2] // 6
    return mod_ref[window, :, number * width : (number + 1) * width]


PLAIN = ((1,), (0,))
RIGHT_T = ((1,), (1,))
LEFT_T = ((0,), (0,))


def qkv_kernel(tokens_ref, mod_ref, w_ref, projected_ref, hidden_ref):
    local = mod_ref.shape[0]
    rows = tokens_ref.shape[0] // local

    @pl.when(pl.program_id(0) == 0)
    def _():
        for window in range(local):
            part = pl.ds(window * rows, rows)
            normed, _ = normalize(tokens_ref[part, :].astype(f32))
            shift, scale = modulation(mod_ref, 0, window), modulation(mod_ref, 1, window)
            hidden_ref[part, :] = (normed * (1.0 + scale) + shift).astype(bf16)

    projected_ref[...] = dot32(hidden_ref[...], w_ref[...], PLAIN).astype(bf16)


def qkv_forward(tokens, mod, w_attn):
    count, width = tokens.shape
    tile = 512
    return dense_call(
        qkv_kernel,
        "qkv",
        (3 * width // tile,),
        [
            full_spec(tokens.shape),
            full_spec(mod.shape),
            pl.BlockSpec((width, tile), lambda i: (0, i)),
        ],
        [pl.BlockSpec((count, tile), lambda i: (0, i)), full_spec(tokens.shape)],
        [jax.ShapeDtypeStruct((count, 3 * width), bf16), jax.ShapeDtypeStruct((count, width), bf16)],
    )(tokens, mod, w_attn)


def out_kernel(attended_ref, w_ref, tokens_ref, mod_ref, branch_ref, mid_ref, hidden_ref):
    branch = dot32(attended_ref[...], w_ref[...], PLAIN)
    mid = tokens_ref[...].astype(f32) + modulation(mod_ref, 2) * branch
    normed, _ = normalize(mid)
    branch_ref[...] = branch.astype(bf16)
    mid_ref[...] = mid
    hidden_ref[...] = (normed * (1.0 + modulation(mod_ref, 4)) + modulation(mod_ref, 3)).astype(bf16)


def out_forward(attended, w_attn, tokens, mod):
    count, width = tokens.shape
    local = mod.shape[0]
    rows = count // local
    row_spec = pl.BlockSpec((rows, width), lambda i: (i, 0))
    return dense_call(
        out_kernel,
        "attn_out",
        (local,),
        [
            row_spec,
            full_spec((width, width)),
            row_spec,
            pl.BlockSpec((1,) + mod.shape[1:], lambda i: (i, 0, 0)),
        ],
        [row_spec] * 3,
        [
            jax.ShapeDtypeStruct((count, width), bf16),
            jax.ShapeDtypeStruct((count, width), f32),
            jax.ShapeDtypeStruct((count, width), bf16),
        ],
    )(attended, w_attn, tokens, mod)


def gelu_parts(value):
    factor = 0.7978845608028654
    square = value * value
    half = 0.5 + 0.5 * jnp.tanh(value * (factor + (factor * 0.044715) * square))
    gelu = value * half
    slope = half + gelu * (1.0 - half) * (2.0 * factor + (6.0 * factor * 0.044715) * square)
    return gelu, slope


def joined(refs, axis):
    parts = [ref[...] for ref in refs]
    return parts[0] if len(parts) == 1 else jnp.concatenate(parts, axis=axis)


def hidden_specs(width, tile, part, fast, rows):
    if not fast:
        return [pl.BlockSpec((rows, tile), lambda i, where: (0, 2 * part + i))]

    def block(z):
        def index(i, where):
            j, l = 1 - part, 1 - i
            return 0, z * 4 + (where[1] ^ j) * 2 + (where[2] ^ l)

        return pl.BlockSpec((rows, tile // 4), index)

    return [block(z) for z in range(4)]


def held_spec(shape):
    return pl.BlockSpec(shape, lambda i, where: (0,) * len(shape))


def hidden_call(kernel, name, where, inputs, in_specs, out_specs, out_shape, scratch=()):
    return pl.pallas_call(
        kernel,
        grid_spec=pltpu.PrefetchScalarGridSpec(
            num_scalar_prefetch=1,
            grid=(2,),
            in_specs=in_specs,
            out_specs=out_specs,
            scratch_shapes=list(scratch),
        ),
        out_shape=in_hbm(out_shape),
        compiler_params=pltpu.CompilerParams(vmem_limit_bytes=VMEM_LIMIT),
        cost_estimate=SMALL,
        name=name,
    )(where, *inputs)


def write_quarters(refs, value):
    @pl.when(pl.program_id(0) == 0)
    def _():
        start = 0
        for ref in refs[:-1]:
            ref[...] = value[start : start + ref.shape[0]].astype(bf16)
            start += ref.shape[0]

    @pl.when(pl.program_id(0) == 1)
    def _():
        refs[-1][...] = value.astype(bf16)


def quarter_shapes(tile, width, part):
    cut = FAR_CUT * tile // 4
    return [(tile, width)] * 2 if part else [(cut, width), (tile - cut, width), (tile, width)]


def up_kernel(pieces, where_ref, own_ref, other_ref, mlp_ref, mlp_other_ref, *refs):
    w, bias = joined(refs[:pieces], 1), joined(refs[pieces : 2 * pieces], 1)
    act_ref, slope_ref = refs[2 * pieces : 2 * pieces + 2]
    grad_refs = refs[2 * pieces + 2 :]
    total = None
    for half, (hidden, mlp) in enumerate(((own_ref, mlp_ref), (other_ref, mlp_other_ref))):
        activated, slope = gelu_parts(dot32(hidden[...], w, PLAIN) + bias)
        activated = activated.astype(bf16)
        act_ref[half] = activated
        slope_ref[half] = slope.astype(bf16)
        part = dot32(activated, mlp[...], LEFT_T)
        total = part if total is None else total + part
    write_quarters(grad_refs, total)


def up_forward(where, rows_both, w_up, bias, part, fast):
    count, width = rows_both[0].shape
    inner = w_up.shape[1]
    tile = inner // 4
    both = pl.BlockSpec((2, count, tile), lambda i, where: (0, 0, i))
    w_specs = hidden_specs(width, tile, part, fast, width)
    bias_specs = hidden_specs(width, tile, part, fast, 1)
    pieces = len(w_specs)
    return hidden_call(
        functools.partial(up_kernel, pieces),
        "mlp_up",
        where,
        list(rows_both) + [w_up] * pieces + [bias] * pieces,
        [held_spec((count, width))] * 4 + w_specs + bias_specs,
        [both, both] + [held_spec(shape) for shape in quarter_shapes(tile, width, part)],
        [low_shape(2, count, 2 * tile)] * 2
        + [low_shape(*shape) for shape in quarter_shapes(tile, width, part)],
    )


def down_back_kernel(pieces, part, where_ref, own_ref, other_ref, mlp_ref, mlp_other_ref, down_ref, *refs):
    up = joined(refs[:pieces], 1)
    slope_ref = refs[pieces]
    refs = refs[pieces + 1 :]
    earlier_ref = refs[0] if part else None
    outs = refs[1:] if part else refs
    quarters = 2 if part else 3
    grad_refs, bias_ref = outs[:quarters], outs[quarters]
    back_refs, total_ref = outs[quarters + 1 : -1], outs[-1]
    step = pl.program_id(0)
    down = down_ref[...]
    total, sums = None, None
    for half, (hidden, mlp) in enumerate(((own_ref, mlp_ref), (other_ref, mlp_other_ref))):
        grad_pre = dot32(mlp[...], down, RIGHT_T) * slope_ref[half].astype(f32)
        column = jnp.sum(grad_pre, axis=0, keepdims=True)
        grad_pre = grad_pre.astype(bf16)
        add = dot32(grad_pre, hidden[...], LEFT_T)
        total = add if total is None else total + add
        sums = column if sums is None else sums + column
        back = dot32(grad_pre, up, RIGHT_T)

        @pl.when(step == 0)
        def _(half=half, back=back):
            total_ref[half] = back + earlier_ref[half].astype(f32) if part else back

        @pl.when(step > 0)
        def _(half=half, back=back):
            total_ref[half] += back

    bias_ref[...] = sums
    write_quarters(grad_refs, total)

    @pl.when(step == 1)
    def _():
        if part:
            back_refs[0][...] = total_ref[0]
            back_refs[1][...] = total_ref[1].astype(bf16)
        else:
            back_refs[0][...] = total_ref[...].astype(bf16)


def down_backward(where, rows_both, w_down, w_up, slope, part, earlier, fast):
    count, width = rows_both[0].shape
    inner = w_up.shape[1]
    tile = inner // 4
    back_shape = (2, count, width)
    if part:
        back_specs = [held_spec((count, width))] * 2
        back_shapes = [jax.ShapeDtypeStruct((count, width), f32), low_shape(count, width)]
    else:
        back_specs = [held_spec(back_shape)]
        back_shapes = [low_shape(*back_shape)]
    w_specs = hidden_specs(width, tile, part, fast, width)
    pieces = len(w_specs)
    return hidden_call(
        functools.partial(down_back_kernel, pieces, part),
        "mlp_back",
        where,
        list(rows_both) + [w_down] + [w_up] * pieces + [slope] + ([earlier] if part else []),
        [held_spec((count, width))] * 4
        + [pl.BlockSpec((tile, width), lambda i, where: (2 * part + i, 0))]
        + w_specs
        + [pl.BlockSpec((2, count, tile), lambda i, where: (0, 0, i))]
        + ([held_spec(back_shape)] if part else []),
        [held_spec(shape) for shape in quarter_shapes(tile, width, part)]
        + [pl.BlockSpec((1, tile), lambda i, where: (0, i))]
        + back_specs,
        [low_shape(*shape) for shape in quarter_shapes(tile, width, part)]
        + [jax.ShapeDtypeStruct((1, 2 * tile), f32)]
        + back_shapes,
        [pltpu.VMEM(back_shape, f32)],
    )


def down_kernel(first_ref, second_ref, w_ref, own_ref, other_ref):
    half = first_ref.shape[2]
    for number, out_ref in enumerate((own_ref, other_ref)):
        total = dot32(first_ref[number], w_ref[:half], PLAIN)
        total = total + dot32(second_ref[number], w_ref[half:], PLAIN)
        out_ref[...] = total.astype(out_ref.dtype)


def down_forward(first, second, w_down):
    _, count, half = first.shape
    width = w_down.shape[1]
    tile = 256
    row_spec = pl.BlockSpec((count, tile), lambda i: (0, i))
    return dense_call(
        down_kernel,
        "mlp_down",
        (width // tile,),
        [full_spec(first.shape)] * 2 + [pl.BlockSpec((2 * half, tile), lambda i: (0, i))],
        [row_spec, row_spec],
        [jax.ShapeDtypeStruct((count, width), f32), low_shape(count, width)],
    )(first, second, w_down)


def split_away(where_ref, rows_ref, away_ref):
    first = pl.multiple_of((1 - where_ref[2]) * 2 * SPATIAL, 2 * SPATIAL)
    away_ref[: 2 * SPATIAL] = rows_ref[pl.ds(first, 2 * SPATIAL), :]
    away_ref[2 * SPATIAL :] = rows_ref[4 * SPATIAL :, :]


def result_kernel(
    where_ref, own_ref, other_ref, bias_ref, mid_ref, cot_ref, mod_ref, live_ref,
    result_ref, away_ref, gate_ref,
):
    branch = own_ref[...] + other_ref[...].astype(f32) + bias_ref[...]
    result_ref[...] = (mid_ref[...] + modulation(mod_ref, 5) * branch).astype(bf16)
    split_away(where_ref, result_ref, away_ref)
    gate_ref[0] = live_ref[0] * jnp.sum(branch * cot_ref[...].astype(f32), axis=0, keepdims=True)


def result_forward(where, own, other, bias, mid, cotangent, mod, live):
    count, width = own.shape
    local = mod.shape[0]
    row_spec = pl.BlockSpec((count // local, width), lambda i: (i, 0))
    one = pl.BlockSpec((1, 1, width), lambda i: (i, 0, 0))
    return dense_call(
        result_kernel,
        "result",
        (local,),
        [pl.BlockSpec(memory_space=pltpu.SMEM)]
        + [row_spec, row_spec, full_spec(bias.shape), row_spec, row_spec]
        + [pl.BlockSpec((1,) + mod.shape[1:], lambda i: (i, 0, 0)), one],
        [row_spec, pl.BlockSpec((3 * SPATIAL, width), lambda i: (i, 0)), one],
        [
            low_shape(count, width),
            low_shape(local * 3 * SPATIAL, width),
            jax.ShapeDtypeStruct((local, 1, width), f32),
        ],
    )(where, own, other, bias, mid, cotangent, mod, live)


def mid_back_kernel(
    own_ref, other_ref, mid_ref, cot_ref, branch_ref, attended_ref, w_ref, mod_ref, live_ref,
    grad_mid_ref, grad_attended_ref, sums_ref, grad_ref, total_ref,
):
    step, last = pl.program_id(0), pl.num_programs(0) - 1
    grad_hidden = own_ref[...] + other_ref[...].astype(f32)
    normed, inverse = normalize(mid_ref[...])
    back = normalize_back(grad_hidden * (1.0 + modulation(mod_ref, 4)), normed, inverse)
    grad_mid = cot_ref[...].astype(f32) + back
    grad_mid_ref[...] = grad_mid
    gate = jnp.sum(branch_ref[...].astype(f32) * grad_mid, axis=0, keepdims=True)
    sums_ref[0, 0:1] = live_ref[0] * gate
    sums_ref[0, 1:2] = jnp.sum(grad_hidden, axis=0, keepdims=True)
    sums_ref[0, 2:3] = jnp.sum(grad_hidden * normed, axis=0, keepdims=True)
    grad_branch = (modulation(mod_ref, 2) * grad_mid).astype(bf16)
    grad_attended_ref[...] = dot32(grad_branch, w_ref[...], RIGHT_T).astype(bf16)
    part = dot32(grad_branch, attended_ref[...], LEFT_T)

    @pl.when(step == 0)
    def _():
        total_ref[...] = part

    @pl.when(step > 0)
    def _():
        total_ref[...] += part

    @pl.when(step == last)
    def _():
        grad_ref[...] = total_ref[...].astype(bf16)


def mid_backward(own, other, mid, cotangent, branch, attended, w_attn, mod, live):
    count, width = own.shape
    local = mod.shape[0]
    row_spec = pl.BlockSpec((count // local, width), lambda i: (i, 0))
    return dense_call(
        mid_back_kernel,
        "mid_back",
        (local,),
        [row_spec] * 6
        + [
            full_spec((width, width)),
            pl.BlockSpec((1,) + mod.shape[1:], lambda i: (i, 0, 0)),
            pl.BlockSpec((1, 1, width), lambda i: (i, 0, 0)),
        ],
        [
            row_spec,
            row_spec,
            pl.BlockSpec((1, 8, width), lambda i: (i, 0, 0)),
            full_spec((width, width)),
        ],
        [
            jax.ShapeDtypeStruct((count, width), f32),
            jax.ShapeDtypeStruct((count, width), bf16),
            jax.ShapeDtypeStruct((local, 8, width), f32),
            jax.ShapeDtypeStruct((width, width), bf16),
        ],
        [pltpu.VMEM((width, width), f32)],
    )(own, other, mid, cotangent, branch, attended, w_attn, mod, live)


def grad_pieces(tiles, tile, width):
    block, out_block = tiles * tile // 32, width // 32
    pieces = []
    for number in range(32):
        pieces.append((0, number, None, number * out_block, block, out_block))
        first, rest, to = number * block, block, 0
        while rest:
            size = min(rest, tile - first % tile)
            pieces.append((first // tile, number, first // tile, first % tile, to, size))
            first, rest, to = first + size, rest - size, to + size
    return pieces


def qkv_grad_kernel(pieces, where_ref, grad_ref, hidden_ref, out_grad_ref, *refs):
    outs, whole_ref, sems = refs[:4], refs[4], refs[5]
    x, y, c = where_ref[1], where_ref[2], where_ref[3]
    step, steps = pl.program_id(0), pl.num_programs(0)
    whole_ref[step] = dot32(grad_ref[0], hidden_ref[...], LEFT_T).astype(bf16)

    for now in range(whole_ref.shape[0]):
        for here_x in range(2):
            for here_c in range(2):

                @pl.when((step == now) & (x == here_x) & (c == here_c))
                def _(now=now, here_x=here_x, here_c=here_c):
                    for count, (ready, number, tile, first, start, size) in enumerate(pieces):
                        if ready != now:
                            continue
                        z, l = number // 8, (number // 2 % 2) ^ y
                        j, core = (number // 4 % 2) ^ here_x, (number % 2) ^ here_c
                        rows = pl.ds(first, size)
                        source = out_grad_ref.at[rows] if tile is None else whole_ref.at[tile, rows]
                        place = outs[2 * core + 1 - j].at[1 - l, z, pl.ds(start, size)]
                        pltpu.make_async_copy(source, place, sems.at[count]).start()

    @pl.when(step == steps - 1)
    def _():
        for count, piece in enumerate(pieces):
            place = outs[0].at[0, 0, pl.ds(0, piece[5])]
            pltpu.make_async_copy(place, place, sems.at[count]).wait()


def qkv_grad(where, grad_projected, hidden, grad_out):
    count, width = hidden.shape
    tile = 512
    per = width // tile
    rows = 4 * width // 32
    shape = low_shape(2, 4, rows, width)
    pieces = grad_pieces(3 * per, tile, width)
    return pl.pallas_call(
        functools.partial(qkv_grad_kernel, pieces),
        grid=(3 * per,),
        in_specs=[
            pl.BlockSpec(memory_space=pltpu.SMEM),
            pl.BlockSpec((1, count, tile), lambda i: (i // per, 0, i % per)),
            full_spec(hidden.shape),
            full_spec(grad_out.shape),
        ],
        out_specs=[pl.BlockSpec(memory_space=pl.ANY)] * 4,
        out_shape=[shape] * 4,
        scratch_shapes=[
            pltpu.VMEM((3 * per, tile, width), bf16),
            pltpu.SemaphoreType.DMA((len(pieces),)),
        ],
        compiler_params=pltpu.CompilerParams(vmem_limit_bytes=VMEM_LIMIT),
        cost_estimate=SMALL,
        name="qkv_grad",
    )(where, grad_projected, hidden, grad_out)


def qkv_grad_plain(grad_projected, hidden):
    return lax.dot_general(
        grad_projected, hidden, (((1,), (0,)), ((), ())), preferred_element_type=f32
    ).astype(bf16)


def tokens_back_kernel(
    where_ref, grad_ref, w_ref, tokens_ref, grad_mid_ref, mod_ref, out_ref, away_ref, sums_ref
):
    width = tokens_ref.shape[1]
    grad_hidden = None
    for part in range(3):
        add = dot32(grad_ref[part], w_ref[:, part * width : (part + 1) * width], RIGHT_T)
        grad_hidden = add if grad_hidden is None else grad_hidden + add
    normed, inverse = normalize(tokens_ref[...].astype(f32))
    back = normalize_back(grad_hidden * (1.0 + modulation(mod_ref, 1)), normed, inverse)
    out_ref[...] = (grad_mid_ref[...] + back).astype(bf16)
    split_away(where_ref, out_ref, away_ref)
    sums_ref[0, 0:1] = jnp.sum(grad_hidden, axis=0, keepdims=True)
    sums_ref[0, 1:2] = jnp.sum(grad_hidden * normed, axis=0, keepdims=True)


def tokens_backward(where, grad_projected, w_qkv, tokens, grad_mid, mod):
    count, width = tokens.shape
    local = mod.shape[0]
    rows = count // local
    row_spec = pl.BlockSpec((rows, width), lambda i: (i, 0))
    return dense_call(
        tokens_back_kernel,
        "tokens_back",
        (local,),
        [
            pl.BlockSpec(memory_space=pltpu.SMEM),
            pl.BlockSpec((3, rows, width), lambda i: (0, i, 0)),
            full_spec((width, 3 * width)),
            row_spec,
            row_spec,
            pl.BlockSpec((1,) + mod.shape[1:], lambda i: (i, 0, 0)),
        ],
        [
            row_spec,
            pl.BlockSpec((3 * SPATIAL, width), lambda i: (i, 0)),
            pl.BlockSpec((1, 8, width), lambda i: (i, 0, 0)),
        ],
        [
            low_shape(count, width),
            low_shape(local * 3 * SPATIAL, width),
            jax.ShapeDtypeStruct((local, 8, width), f32),
        ],
    )(where, grad_projected, w_qkv, tokens, grad_mid, mod)


def modulation_kernel(parts_ref, bias_ref, live_ref, out_ref):
    sources, holders, local, part = parts_ref.shape
    width = out_ref.shape[2] // 6
    for window in range(local):
        for holder in range(holders):
            total = parts_ref[0, holder, window : window + 1]
            for source in range(1, sources):
                total = total + parts_ref[source, holder, window : window + 1]
            columns = slice(holder * part, (holder + 1) * part)
            out_ref[window, :, columns] = total + bias_ref[:, columns]
        for gate in (2, 5):
            columns = slice(gate * width, (gate + 1) * width)
            out_ref[window, :, columns] = out_ref[window, :, columns] * live_ref[window]


def modulate(parts, bias, live):
    local, _, width = live.shape
    return dense_call(
        modulation_kernel,
        "modulation",
        (1,),
        [full_spec(parts.shape), full_spec(bias.shape), full_spec(live.shape)],
        full_spec((local, 1, 6 * width)),
        jax.ShapeDtypeStruct((local, 1, 6 * width), f32),
    )(parts, bias, live)


def gated_kernel(where_ref, rows_ref, mod_ref, out_ref):
    out_ref[...] = (modulation(mod_ref, 5) * rows_ref[...].astype(f32)).astype(bf16)


def gated(where, rows, mod):
    count, width = rows.shape
    local = mod.shape[0]
    row_spec = pl.BlockSpec((count // local, width), lambda i: (i, 0))
    return dense_call(
        gated_kernel,
        "gated",
        (local,),
        [
            pl.BlockSpec(memory_space=pltpu.SMEM),
            row_spec,
            pl.BlockSpec((1,) + mod.shape[1:], lambda i: (i, 0, 0)),
        ],
        row_spec,
        low_shape(count, width),
    )(where, rows, mod)


def space_onehot():
    places = jnp.arange(SPATIAL, dtype=jnp.int32)
    across, along = places // SIDE, places % SIDE
    index = (across[:, None] - across[None, :] + SIDE - 1) * (2 * SIDE - 1) + (
        along[:, None] - along[None, :] + SIDE - 1
    )
    ids = jnp.arange((2 * SIDE - 1) ** 2, dtype=jnp.int32)
    return (index.reshape(-1)[:, None] == ids[None, :]).astype(f32)


def on_device(
    tokens,
    condition,
    doubled,
    window_count,
    w_ada,
    b_ada,
    w_qkv,
    w_out,
    w_up,
    b_up,
    w_down,
    b_down,
    table_space,
    table_time,
    cotangent,
):
    windows, _, width = tokens.shape
    heads = table_space.shape[0]
    n_win = lax.axis_size("win")
    devices = n_win * 4
    win = lax.axis_index("win")
    frm = lax.axis_index("frm")
    z, x, y, c = win // 2, win % 2, frm // 2, frm % 2
    where = jnp.concatenate([jnp.stack([z, x, y, c, frm, window_count[0]]), doubled])
    where = where.astype(jnp.int32)
    local = windows // 4
    count = local * FRAMES * SPATIAL
    ff = w_up.shape[1]
    ff_block = ff // devices
    shard_rows = w_qkv.shape[0]
    half_width = width // 2
    fast = n_win == 8
    slot_shape = (2 * windows, SPATIAL, width)

    tok_slots, cot_slots = tokens.reshape(slot_shape), cotangent.reshape(slot_shape)
    tok_send = windows_send(where, tok_slots)
    biases = jnp.concatenate([b_ada, b_up, b_down])
    bias_rows = -(-biases.shape[0] // width)
    biases = jnp.pad(biases, (0, bias_rows * width - biases.shape[0])).reshape(bias_rows, width)
    small = jnp.concatenate([condition, biases])
    if fast:
        q_half, up_half, down_half = halves(where, w_qkv, w_out, w_up, w_down)
        q_direct = gather_z_direct(q_half)
        tok_send, _ = sync(tok_send, q_half)
        small, _ = sync(small, tok_send)
    small_all = lax.all_to_all(
        jnp.broadcast_to(small[None], (n_win,) + small.shape),
        "win",
        split_axis=0,
        concat_axis=0,
        tiled=True,
    )
    tok_got = swap_core(tok_send)
    tok_here, tok_away = windows_pack(where, tok_slots, tok_got)
    tok_back = swap_y(tok_away)

    onehot_space = space_onehot()
    space_bias = jnp.dot(table_space, onehot_space.T, precision=exact_mode)
    space_bias = jnp.tile(space_bias.reshape(heads, SPATIAL, SPATIAL), (1, 1, FRAMES))
    mine_doubled = lax.dynamic_slice_in_dim(doubled, frm * local, local, 0)
    holders = jnp.arange(4, dtype=jnp.int32)
    frames = holders[None, :] + (holders[None, :] > mine_doubled[:, None]).astype(jnp.int32)
    frames = jnp.concatenate([frames, mine_doubled[:, None] + 1], axis=1)
    offset = frames[:, :, None] - frames[:, None, :] + FRAMES - 1
    onehot_time = (
        offset[..., None] == jnp.arange(table_time.shape[1], dtype=jnp.int32)
    ).astype(f32)
    time_bias = jnp.einsum("wabt,ht->whab", onehot_time, table_time, precision=exact_mode)
    time_bias = jnp.repeat(time_bias, SPATIAL, axis=-1)
    time_bias = jnp.pad(time_bias, ((0, 0), (0, 0), (0, 8 - FRAMES), (0, 0)))

    if fast:
        *q_direct, _ = sync(*q_direct, tok_away)
        q_stack = jnp.stack(q_direct)
        q_near = gather_near(q_stack)
        small_all, up_half, _ = sync(small_all, up_half, q_stack)
        up_direct = gather_z_direct(up_half)

    cond_all = small_all[:, :windows].reshape(n_win * windows, width).astype(f32)
    bias_all = small_all[:, windows:].reshape(n_win, bias_rows * width).astype(f32)
    cuts = [b_ada.shape[0], b_ada.shape[0] + b_up.shape[0]]
    ada_bias = bias_all[:, : cuts[0]].reshape(1, 6 * width)
    up_bias = bias_all[:, cuts[0] : cuts[1]].reshape(n_win * 2, 2, ff_block)
    up_bias = pick(up_bias, c, 1).reshape(1, ff // 2)
    down_bias = bias_all[:, cuts[1] : cuts[1] + b_down.shape[0]].reshape(1, width)
    silu_all = jax.nn.silu(cond_all).astype(bf16)
    silu_part = lax.dynamic_slice_in_dim(silu_all, win * shard_rows, shard_rows, 1)
    ada_quarter = 6 * width // 4
    ada_part = lax.dynamic_slice_in_dim(w_ada, frm * ada_quarter, ada_quarter, 1)
    mod_part = dot32(silu_part, ada_part, PLAIN)
    if fast:
        *q_near, mod_part, up_bias, down_bias, space_bias, time_bias = sync(
            *q_near, mod_part, up_bias, down_bias, space_bias, time_bias
        )
        q_far = gather_far(q_near)
        *up_direct, q_near[0], q_near[1], q_near[2] = sync(*up_direct, *q_near)
        q_other = [swap_core(part) for part in q_near]
    else:
        qkv_full = lax.all_gather(w_qkv, "win", axis=0).reshape(width, 3 * width)
        out_full = lax.all_gather(w_out, "win", axis=0).reshape(width, width)
        up_shard = pick(w_up.reshape(shard_rows, n_win * 2, 2, ff_block), c, 2)
        up_full = lax.all_gather(up_shard, "win", axis=0).reshape(width, ff // 2)
        down_shard = pick(w_down.reshape(2, 2, ff_block, width), c, 1)
        down_full = lax.all_gather(down_shard, "win", axis=0).reshape(ff // 2, width)
    mod_parts = exchange_all(mod_part.reshape(devices, local, ada_quarter))
    my_window = frm * local + jnp.arange(local, dtype=jnp.int32)
    live = (my_window < window_count[0]).astype(f32)[:, None, None]
    live = jnp.broadcast_to(live, (local, 1, width))
    cot_send = windows_send(where, cot_slots)
    if fast:
        up_stack = jnp.stack(up_direct)
        q_far[0], tok_back, mod_parts, cot_send, up_stack, *q_other = sync(
            q_far[0], tok_back, mod_parts, cot_send, up_stack, *q_other
        )
        q_other = q_other + [swap_core(part) for part in q_far]
        up_near = gather_near(up_stack)
        qkv_full, out_full = place_qkv(where, list(q_near) + list(q_far) + q_other)
    cot_got = swap_core(cot_send)
    token_rows = windows_join(where, tok_here, tok_back)
    mod = modulate(mod_parts.reshape(n_win, 4, local, ada_quarter), ada_bias, live)

    projected, hidden_one = qkv_forward(token_rows, mod, qkv_full)
    cot_here, cot_away = windows_pack(where, cot_slots, cot_got)
    if fast:
        projected, cot_away, down_half, *up_near = sync(
            projected, cot_away, down_half, *up_near
        )
        up_far = gather_far(up_near)
        down_direct = gather_z_direct(down_half)
    cot_back = swap_y(cot_away)
    attended, probs = attend(projected, space_bias, time_bias, local)
    if fast:
        attended, cot_back, up_far[0], *down_direct = sync(
            attended, cot_back, up_far[0], *down_direct
        )
        down_near = gather_near(jnp.stack(down_direct))
    branch_attn, mid, hidden_two = out_forward(attended, out_full, token_rows, mod)
    grad_out = windows_join(where, cot_here, cot_back)
    grad_mlp = gated(where, grad_out, mod)
    mlp_other = swap_core(grad_mlp)

    hidden_other = swap_core(hidden_two)
    if fast:
        up_full = place_up(where, list(up_near) + list(up_far))
    rows_both = (hidden_two, hidden_other, grad_mlp, mlp_other)
    act_first, slope_first, *down_grads = up_forward(where, rows_both, up_full, up_bias, 0, fast)
    if fast:
        act_first, up_bias, *down_near = sync(act_first, up_bias, *down_near)
        down_far = gather_far(down_near, FAR_CUT)
    act_second, slope_second, *more = up_forward(where, rows_both, up_full, up_bias, 1, fast)
    if fast:
        act_second, *down_far = sync(act_second, *down_far)
        down_fy, down_fx = swap_y(down_grads[0]), swap_win(down_grads[1], 1)
        down_full = place_down(where, list(down_near) + list(down_far))
    down_grads = list(down_grads) + more
    block_rows = ff_block
    *up_grads, up_b_first, back_first = down_backward(
        where, rows_both, down_full, up_full, slope_first, 0, None, fast
    )
    if fast:
        back_first, *up_grads, down_fy, down_fx = sync(back_first, *up_grads, down_fy, down_fx)
        send_x, send_y = merge(
            [(down_grads[2], None)], [(down_grads[3], None)], down_fy, down_fx
        )
        back_first, send_x, send_y = sync(back_first, send_x, send_y)
        down_x, down_y = swap_win(send_x, 1), swap_y(send_y)
    *more, up_b_second, back_own, back_other = down_backward(
        where, rows_both, down_full, up_full, slope_second, 1, back_first, fast
    )
    up_grads = list(up_grads) + more
    if fast:
        back_other, act_first, down_x, down_y = sync(back_other, act_first, down_x, down_y)
        up_fy, up_fx = swap_y(up_grads[0]), swap_win(up_grads[1], 1)
        down_kept = total(
            [(down_grads[4], None), (down_x, None), (down_y, None)], block_rows, width
        )
    back_got = swap_core(back_other)
    mlp_own, mlp_away = down_forward(act_first, act_second, down_full)

    if fast:
        back_got, mlp_away, down_kept, *up_grads, up_fy, up_fx = sync(
            back_got, mlp_away, down_kept, *up_grads, up_fy, up_fx
        )
        down_parts = parts_z(down_kept)
        send_x, send_y = merge([(up_grads[2], None)], [(up_grads[3], None)], up_fy, up_fx)
        back_got, send_x, send_y = sync(back_got, send_x, send_y)
        up_x, up_y = swap_win(send_x, 1), swap_y(send_y)
    mlp_got = swap_core(mlp_away)
    grad_mid, grad_attended, mid_sums, grad_out_w = mid_backward(
        back_own, back_got, mid, grad_out, branch_attn, attended, out_full, mod, live
    )
    grad_attended, mlp_got = sync(grad_attended, mlp_got)
    result, res_away, gate_two_sum = result_forward(
        where, mlp_own, mlp_got, down_bias, mid, grad_out, mod, live
    )
    grad_attended, res_away = sync(grad_attended, res_away)
    res_back = swap_y(res_away.reshape(6, SPATIAL, width))
    grad_projected, space_sums, time_sums = attend_back(
        projected, grad_attended, attended, probs, local
    )
    qkv_block, out_block = 3 * width // devices, width // devices
    if fast:
        grad_projected, up_x, up_y, res_back, down_parts = sync(
            grad_projected, up_x, up_y, res_back, down_parts
        )
        own_first, own_second, other_first, other_second = qkv_grad(
            where, grad_projected, hidden_one, grad_out_w
        )
        up_x, other_first, other_second = sync(up_x, other_first, other_second)
        up_kept = total([(up_grads[4], None), (up_x, None), (up_y, None)], block_rows, width)
        up_grad = add_z(parts_z(up_kept))
        got_first, got_second = swap_core(other_first), swap_core(other_second)
    if fast:
        got_first, up_kept = sync(got_first, up_kept)
        send_fy, send_fx, attn_gx = first_quarters(own_first, got_first)
        send_fy, send_fx, grad_projected = sync(send_fy, send_fx, grad_projected)
        attn_fy, attn_fx = swap_y(send_fy), swap_win(send_fx, 1)
    else:
        grad_attn_w = jnp.concatenate(
            [
                qkv_grad_plain(grad_projected, hidden_one).reshape(n_win, 2, 2, qkv_block, width),
                grad_out_w.reshape(n_win, 2, 2, out_block, width),
            ],
            axis=3,
        )
        got = swap_core(pick(grad_attn_w, 1 - c, 2))
        attn_grad = scatter_plain(add_low(pick(grad_attn_w, c, 2), got), where)
        up_grad = scatter_plain(jnp.concatenate(up_grads).reshape(n_win, 2, ff_block, width), where)
        down_grad = scatter_plain(
            jnp.concatenate(down_grads).reshape(n_win, 2, ff_block, width), where
        )
    grad_tokens, gt_away, token_sums = tokens_backward(
        where, grad_projected, qkv_full, token_rows, grad_mid, mod
    )
    gt_away = gt_away.reshape(6, SPATIAL, width)
    if fast:
        token_sums, attn_fy, attn_fx, got_second = sync(
            token_sums, attn_fy, attn_fx, got_second
        )
        send_x, send_y = merge(
            [(attn_gx, None)], [(own_second, 0), (got_second, 0)], attn_fy, attn_fx, LAST_CUT
        )
        attn_x, attn_y = swap_win(send_x, 1), swap_y(send_y)
        token_sums, res_back, _, _ = sync(token_sums, res_back, send_x, send_y)

    grad_mod = jnp.concatenate(
        [
            token_sums[:, 0],
            token_sums[:, 1],
            mid_sums[:, 0],
            mid_sums[:, 1],
            mid_sums[:, 2],
            gate_two_sum[:, 0],
        ],
        axis=-1,
    ).astype(bf16)
    ada_block = 6 * width // devices
    to_quarter = jnp.transpose(grad_mod.reshape(local, 4, ada_quarter), (1, 0, 2))
    to_quarter = jnp.broadcast_to(to_quarter[None], (n_win, 4, local, ada_quarter))
    to_block = jnp.transpose(grad_mod.reshape(local, devices, ada_block), (1, 0, 2))
    grad_up_b = jnp.concatenate([up_b_first, up_b_second], axis=1)
    if fast:
        grad_up_b = grad_up_b.reshape(2, 2, 4, ff_block)
        grad_up_b = jnp.where(x == 0, grad_up_b[::-1], grad_up_b)
        grad_up_b = jnp.where(y == 0, grad_up_b[:, ::-1], grad_up_b)
        grad_up_b = jnp.transpose(grad_up_b, (2, 0, 1, 3))
    grad_up_b = grad_up_b.reshape(n_win * 2, 1, ff_block)
    core_mask = (jnp.arange(2, dtype=jnp.int32) == c).astype(f32)[None, :, None]
    grad_up_b = (grad_up_b * core_mask).reshape(devices, ff_block)
    grad_down_b = jnp.sum(grad_mlp.astype(f32), axis=0).reshape(devices, width // devices)
    first_send = jnp.concatenate(
        [
            to_quarter.reshape(devices, local * ada_quarter),
            to_block.reshape(devices, local * ada_block),
            grad_up_b.astype(bf16),
            grad_down_b.astype(bf16),
        ],
        axis=1,
    )
    res_other = swap_core(windows_back_pack(where, result, res_back))
    first_got = exchange_all(first_send)
    if fast:
        down_grad = add_z(down_parts)
        attn_x, attn_y, gt_away, res_other, first_send = sync(
            attn_x, attn_y, gt_away, res_other, first_send
        )
        kept = total(
            [(own_second, 1), (got_second, 1), (attn_x, None), (attn_y, None)],
            qkv_block + out_block,
            width,
        )
        attn_grad = sum_z_direct(kept, z)
        first_got, _ = sync(first_got, kept)
    gt_back = swap_y(gt_away)
    if fast:
        space_sums, time_sums, gt_back = sync(space_sums, time_sums, gt_back)
    lanes = jnp.arange(FRAMES * SPATIAL, dtype=jnp.int32)
    to_place = (lanes[:, None] % SPATIAL == jnp.arange(SPATIAL)[None]).astype(f32)
    to_slot = (lanes[:, None] // SPATIAL == jnp.arange(FRAMES)[None]).astype(f32)
    space_sum = jnp.dot(
        space_sums.reshape(heads * SPATIAL, FRAMES * SPATIAL), to_place, precision=exact_mode
    )
    space_sum = jnp.dot(
        space_sum.reshape(heads, SPATIAL * SPATIAL), onehot_space, precision=exact_mode
    )
    time_sum = jnp.dot(
        time_sums.reshape(local * heads * 8, FRAMES * SPATIAL), to_slot, precision=exact_mode
    ).reshape(local, heads, 8, FRAMES)[:, :, :FRAMES]
    time_sum = jnp.einsum("whab,wabt->ht", time_sum, onehot_time, precision=exact_mode)
    tables = jnp.concatenate([space_sum.reshape(-1), time_sum.reshape(-1)])
    sizes = [local * ada_quarter, local * ada_block, ff_block, width // devices]
    ends = [sum(sizes[: n + 1]) for n in range(4)]
    mod_got = first_got[:, : ends[0]].reshape(n_win * windows, ada_quarter)
    mod_own = first_got[:, ends[0] : ends[1]].reshape(n_win * windows, ada_block)
    sums = jnp.sum(first_got[:, ends[1] :].astype(f32), axis=0)
    out_up_b = sums[:ff_block]
    out_down_b = sums[ff_block : ff_block + width // devices]
    grad_ada_w = dot32(silu_all, mod_own, LEFT_T)
    grad_ada_b = jnp.sum(mod_own.astype(f32), axis=0)
    cond_part = dot32(mod_got, ada_part, RIGHT_T)
    cond_send = cond_part.astype(bf16).reshape(n_win, 1, windows * shard_rows)
    cond_send = jnp.broadcast_to(cond_send, (n_win, 4, windows * shard_rows))
    cond_send = cond_send.reshape(devices, windows * shard_rows)
    table_send = jnp.broadcast_to(tables.astype(bf16)[None], (devices, tables.shape[0]))
    last_got = exchange_all(jnp.concatenate([cond_send, table_send], axis=1)).astype(f32)
    cond_grad = last_got[:, : windows * shard_rows].reshape(n_win, 4, windows, shard_rows)
    cond_grad = jnp.transpose(jnp.sum(cond_grad, axis=1), (1, 0, 2)).reshape(windows, width)
    _, silu_back = jax.vjp(jax.nn.silu, condition.astype(f32))
    grad_condition = silu_back(cond_grad)[0]
    table_all = jnp.sum(last_got[:, windows * shard_rows :], axis=0)
    space_size = table_space.size
    grad_space = table_all[:space_size].reshape(table_space.shape)
    grad_time = table_all[space_size : space_size + table_time.size].reshape(table_time.shape)

    gt_other = swap_core(windows_back_pack(where, grad_tokens, gt_back))
    result = windows_back_join(where, result, res_back, res_other, tokens, bf16)
    grad_tokens = windows_back_join(where, grad_tokens, gt_back, gt_other, cotangent, f32)

    return (
        result,
        grad_tokens,
        grad_condition,
        grad_ada_w,
        grad_ada_b,
        attn_grad[:qkv_block].T,
        attn_grad[qkv_block:].T,
        up_grad.T,
        out_up_b,
        down_grad,
        out_down_b,
        grad_space,
        grad_time,
    )


def solution(mesh):
    return jax.shard_map(
        on_device,
        mesh=mesh,
        in_specs=(
            P("win", "frm", None),
            P("win", None),
            P("win"),
            P("win"),
            P("win", None),
            P("win"),
            P("win", None),
            P("win", None),
            P("win", None),
            P("win"),
            P("win", None),
            P("win"),
            P(),
            P(),
            P("win", "frm", None),
        ),
        out_specs=(
            P("win", "frm", None),
            P("win", "frm", None),
            P("win", None),
            P(None, BOTH),
            P(BOTH),
            P(None, BOTH),
            P(None, BOTH),
            P(None, BOTH),
            P(BOTH),
            P(BOTH, None),
            P(BOTH),
            P(),
            P(),
        ),
        check_vma=False,
    )
```

profile of v0, /device:TPU:9, one launch (start us, length us, event | category | flops | bytes accessed | tf_op | source)
XLA Modules:
  0.0 473.1 jit_solution(17806456166790705078)
XLA Ops:
  2.7 3.0 halves.1
  8.5 3.0 rows_send.2
  13.9 6.6 %all-to-all-start = ((bf16[8,10,1024]{2,1,0:T(8,128)(2,1)}), bf16[8,10,1024]{2,1,0:T(8,128)(2,1)}, u32[]{:S(2)}, u32[]{:S(2)}) async-start(bf16[8,10,1024]{2,1,0:T(8,128)(2,1)} %broadcast_in_dim.14), calls=%async_computation | async-start | bytes 524288 | tf_op jit(solution)/shard_map/all_to_all | solution.py:1195
  21.2 3.4 rows_pack.2
  24.7 9.4 %collective-permute-done.3 = bf16[32,4096]{1,0:T(8,128)(2,1)} collective-permute-done((bf16[32,4096]{1,0:T(8,128)(2,1)}, bf16[32,4096]{1,0:T(8,128)(2,1)}, u32[]{:S(2)}, u32[]{:S(2)}) %collective-permute-start.3) | collective-permute-done | bytes 262176 | tf_op jit(solution)/shard_map/ppermute | solution.py:38
  40.8 2.6 convolution_bitcast_fusion
  52.0 5.4 %collective-permute-done.4.refs_1_ = bf16[4,32,4096]{2,1,0:T(8,128)(2,1)} collective-permute-done((bf16[4,32,4096]{2,1,0:T(8,128)(2,1)S(1)}, bf16[4,32,4096]{2,1,0:T(8,128)(2,1)}, u32[]{:S(2)}, u32[]{:S(2)}) %collective-permute-start.4) | collective-permute-done | bytes 1048608 | tf_op jit(solution)/shard_map/ppermute | solution.py:38
  59.5 6.7 %collective-permute-done.9 = bf16[64,2048]{1,0:T(8,128)(2,1)} collective-permute-done((bf16[64,2048]{1,0:T(8,128)(2,1)}, bf16[64,2048]{1,0:T(8,128)(2,1)}, u32[]{:S(2)}, u32[]{:S(2)}) %collective-permute-start.9) | collective-permute-done | bytes 262176 | tf_op jit(solution)/shard_map/ppermute | solution.py:38
  71.6 7.0 %all-to-all-start.1 = ((f32[32,2,1536]{2,1,0:T(2,128)}), f32[32,2,1536]{2,1,0:T(2,128)S(1)}, u32[]{:S(2)}, u32[]{:S(2)}) async-start(f32[32,2,1536]{2,1,0:T(2,128)} %reshape.371), calls=%async_computation.1 | async-start | bytes 786432 | tf_op jit(solution)/shard_map/all_to_all | solution.py:42
  78.6 3.1 rows_send.3
  83.9 7.8 %collective-permute-done.7.refs_1_ = bf16[6,64,1024]{2,1,0:T(8,128)(2,1)} collective-permute-done((bf16[6,64,1024]{2,1,0:T(8,128)(2,1)}, bf16[6,64,1024]{2,1,0:T(8,128)(2,1)}, u32[]{:S(2)}, u32[]{:S(2)}) %collective-permute-start.7) | collective-permute-done | bytes 786464 | tf_op jit(solution)/shard_map/ppermute | solution.py:25
  91.7 6.6 %all-to-all-done.1 = f32[32,2,1536]{2,1,0:T(2,128)S(1)} async-done(((f32[32,2,1536]{2,1,0:T(2,128)}), f32[32,2,1536]{2,1,0:T(2,128)S(1)}, u32[]{:S(2)}, u32[]{:S(2)}) %all-to-all-start.1) | async-done | bytes 393248 | tf_op jit(solution)/shard_map/all_to_all | solution.py:42
  107.0 8.0 %place_qkv.1 = (bf16[8,2,2,32,3072]{4,3,2,1,0:T(8,128)(2,1)}, bf16[8,2,2,32,1024]{4,3,2,1,0:T(8,128)(2,1)}) custom-call(s32[14]{0:T(128)S(1)} %copy-done.46, bf16[4,32,4096]{2,1,0:T(8,128)(2,1)S(1)} %copy-done.13, bf16[4,32,4096]{2,1,0:T(8,128)(2,1)} %collective-permute-done.4.refs_1_, bf16[4,32,4096]{2,1,0:T(8,128)(2,1)} %collective-permute-done.5.refs_2_, ...), custom_call_target="tpu_custom_call" | custom-call | flops 1024 | bytes 1024 | tf_op jit(solution)/shard_map/place_qkv/pallas_call | solution.py:98
  115.1 9.7 %qkv.1 = (bf16[640,3072]{1,0:T(8,128)(2,1)}, bf16[640,1024]{1,0:T(8,128)(2,1)}) custom-call(bf16[640,1024]{1,0:T(8,128)(2,1)S(1)} %bitcast.153, f32[2,1,6144]{2,1,0:T(1,128)S(1)} %copy-done.17, bf16[1024,3072]{1,0:T(8,128)(2,1)} %bitcast.185), custom_call_target="tpu_custom_call" | custom-call | flops 1024 | bytes 1024 | tf_op jit(solution)/shard_map/qkv/pallas_call | solution.py:624
  124.7 3.4 rows_pack.3
  131.8 2.5 collective-permute-start.20
  135.6 3.1 copy.81.space_ref
  140.1 14.4 %attend.1 = (bf16[640,1024]{1,0:T(8,128)(2,1)}, bf16[2,16,320,320]{3,2,1,0:T(8,128)(2,1)}) custom-call(bf16[640,3072]{1,0:T(8,128)(2,1)} %get-tuple-element.217.q_ref.k_ref.v_ref, bf16[640,3072]{1,0:T(8,128)(2,1)} %get-tuple-element.217.q_ref.k_ref.v_ref, bf16[640,3072]{1,0:T(8,128)(2,1)} %get-tuple-element.217.q_ref.k_ref.v_ref, ...), custom_call_target="tpu_custom_call" | custom-call | flops 1024 | bytes 1024 | tf_op jit(solution)/shard_map/attend/pallas_call | solution.py:515
  154.5 3.3 collective-permute-done.22
  161.9 2.5 collective-permute-start.24
  164.4 5.2 %attn_out.1 = (bf16[640,1024]{1,0:T(8,128)(2,1)}, f32[640,1024]{1,0:T(8,128)}, bf16[640,1024]{1,0:T(8,128)(2,1)}) custom-call(bf16[640,1024]{1,0:T(8,128)(2,1)S(1)} %copy-done.7, bf16[1024,1024]{1,0:T(8,128)(2,1)} %bitcast.194, bf16[640,1024]{1,0:T(8,128)(2,1)S(1)} %bitcast.154, f32[2,1,6144]{2,1,0:T(1,128)S(1)} %copy-done.17), custom_call_target="tpu_custom_call" | custom-call | flops 1024 | bytes 1024 | tf_op jit(solution)/shard_map/attn_out/pallas_call | solution.py:652
  173.0 4.4 place_up.1
  178.5 13.0 %mlp_up.2 = (bf16[2,640,1024]{2,1,0:T(8,128)(2,1)}, bf16[2,640,1024]{2,1,0:T(8,128)(2,1)}, bf16[256,1024]{1,0:T(8,128)(2,1)}, bf16[256,1024]{1,0:T(8,128)(2,1)}, bf16[512,1024]{1,0:T(8,128)(2,1)}) custom-call(s32[14]{0:T(128)S(1)} %copy-done.46, bf16[640,1024]{1,0:T(8,128)(2,1)S(1)} %copy-done.2, bf16[640,1024]{1,0:T(8,128)(2,1)S(1)} %collective-permute-done.23.other_ref, ...), custom_call_target="tpu_custom_call" | custom-call | flops 1024 | bytes 1024 | tf_op jit(solution)/shard_map/mlp_up/pallas_call | solution.py:704
  191.5 4.1 collective-permute-done.25.refs_1_
  198.9 13.1 %mlp_up.3 = (bf16[2,640,1024]{2,1,0:T(8,128)(2,1)}, bf16[2,640,1024]{2,1,0:T(8,128)(2,1)}, bf16[512,1024]{1,0:T(8,128)(2,1)}, bf16[512,1024]{1,0:T(8,128)(2,1)}) custom-call(s32[14]{0:T(128)S(1)} %copy-done.46, bf16[640,1024]{1,0:T(8,128)(2,1)S(1)} %copy-done.2, bf16[640,1024]{1,0:T(8,128)(2,1)S(1)} %collective-permute-done.23.other_ref, ...), custom_call_target="tpu_custom_call" | custom-call | flops 1024 | bytes 1024 | tf_op jit(solution)/shard_map/mlp_up/pallas_call | solution.py:704
  212.1 4.0 place_down.1
  216.1 16.8 %mlp_back.2 = (bf16[256,1024]{1,0:T(8,128)(2,1)}, bf16[256,1024]{1,0:T(8,128)(2,1)}, bf16[512,1024]{1,0:T(8,128)(2,1)}, f32[1,1024]{1,0:T(1,128)}, bf16[2,640,1024]{2,1,0:T(8,128)(2,1)}) custom-call(s32[14]{0:T(128)S(1)} %copy-done.46, bf16[640,1024]{1,0:T(8,128)(2,1)S(1)} %copy-done.2, bf16[640,1024]{1,0:T(8,128)(2,1)S(1)} %collective-permute-done.23.other_ref, ...), custom_call_target="tpu_custom_call" | custom-call | flops 1024 | bytes 1024 | tf_op jit(solution)/shard_map/mlp_back/pallas_call | solution.py:704
  236.6 18.2 %mlp_back.3 = (bf16[512,1024]{1,0:T(8,128)(2,1)}, bf16[512,1024]{1,0:T(8,128)(2,1)}, f32[1,1024]{1,0:T(1,128)}, f32[640,1024]{1,0:T(8,128)}, bf16[640,1024]{1,0:T(8,128)(2,1)}) custom-call(s32[14]{0:T(128)S(1)} %copy-done.46, bf16[640,1024]{1,0:T(8,128)(2,1)S(1)} %copy-done.2, bf16[640,1024]{1,0:T(8,128)(2,1)S(1)} %collective-permute-done.23.other_ref, ...), custom_call_target="tpu_custom_call" | custom-call | flops 1024 | bytes 1024 | tf_op jit(solution)/shard_map/mlp_back/pallas_call | solution.py:704
  257.8 3.9 collective-permute-start.33
  263.5 9.2 %mlp_down.1 = (f32[640,1024]{1,0:T(8,128)}, bf16[640,1024]{1,0:T(8,128)(2,1)}) custom-call(bf16[2,640,1024]{2,1,0:T(8,128)(2,1)S(1)} %copy-done.16, bf16[2,640,1024]{2,1,0:T(8,128)(2,1)} %get-tuple-element.266.second_ref, bf16[2048,1024]{1,0:T(8,128)(2,1)} %bitcast.184), custom_call_target="tpu_custom_call" | custom-call | flops 1024 | bytes 1024 | tf_op jit(solution)/shard_map/mlp_down/pallas_call | solution.py:860
  278.6 4.5 all-to-all-start.2
  291.1 12.1 %mid_back.1 = (f32[640,1024]{1,0:T(8,128)}, bf16[640,1024]{1,0:T(8,128)(2,1)}, f32[2,8,1024]{2,1,0:T(8,128)}, bf16[1024,1024]{1,0:T(8,128)(2,1)}) custom-call(f32[640,1024]{1,0:T(8,128)} %get-tuple-element.268.own_ref, bf16[640,1024]{1,0:T(8,128)(2,1)S(1)} %copy-done.24, f32[640,1024]{1,0:T(8,128)} %get-tuple-element.287.mid_ref, ...), custom_call_target="tpu_custom_call" | custom-call | flops 1024 | bytes 1024 | tf_op jit(solution)/shard_map/mid_back/pallas_call | solution.py:942
  303.2 4.6 result.1
  309.1 19.4 %attend_back.1 = (bf16[3,640,1024]{2,1,0:T(8,128)(2,1)}, f32[16,64,320]{2,1,0:T(8,128)}, f32[2,16,8,320]{3,2,1,0:T(8,128)}) custom-call(bf16[640,3072]{1,0:T(8,128)(2,1)} %get-tuple-element.217.q_ref.k_ref.v_ref, bf16[640,3072]{1,0:T(8,128)(2,1)} %get-tuple-element.217.q_ref.k_ref.v_ref, bf16[640,3072]{1,0:T(8,128)(2,1)} %get-tuple-element.217.q_ref.k_ref.v_ref, ...), custom_call_target="tpu_custom_call" | custom-call | flops 1024 | bytes 1024 | tf_op jit(solution)/shard_map/attend_back/pallas_call | solution.py:534
  332.5 13.1 %qkv_grad.1 = (bf16[2,4,128,1024]{3,2,1,0:T(8,128)(2,1)S(1)}, bf16[2,4,128,1024]{3,2,1,0:T(8,128)(2,1)}, bf16[2,4,128,1024]{3,2,1,0:T(8,128)(2,1)}, bf16[2,4,128,1024]{3,2,1,0:T(8,128)(2,1)}) custom-call(s32[14]{0:T(128)S(1)} %copy-done.46, bf16[3,640,1024]{2,1,0:T(8,128)(2,1)} %get-tuple-element.317.grad_ref, bf16[640,1024]{1,0:T(8,128)(2,1)S(1)} %copy-done.21, ...), custom_call_target="tpu_custom_call" | custom-call | flops 1024 | bytes 1024 | tf_op jit(solution)/shard_map/qkv_grad/pallas_call | solution.py:1017
  354.2 3.4 first_quarters.1
  359.3 4.5 all-to-all-start.5
  365.6 10.2 %tokens_back.1 = (bf16[640,1024]{1,0:T(8,128)(2,1)}, bf16[384,1024]{1,0:T(8,128)(2,1)}, f32[2,8,1024]{2,1,0:T(8,128)}) custom-call(s32[14]{0:T(128)S(1)} %copy-done.46, bf16[3,640,1024]{2,1,0:T(8,128)(2,1)} %get-tuple-element.317.grad_ref, bf16[1024,3072]{1,0:T(8,128)(2,1)} %bitcast.186, bf16[640,1024]{1,0:T(8,128)(2,1)S(1)} %bitcast.155, ...), custom_call_target="tpu_custom_call" | custom-call | flops 1024 | bytes 1024 | tf_op jit(solution)/shard_map/tokens_back/pallas_call | solution.py:1065
  376.5 4.2 merge.5
  382.2 3.3 rows_back_pack.2
  390.2 3.9 all-to-all-start.3
  398.9 10.5 %all-to-all-done.3 = bf16[32,2,1808]{2,1,0:T(2,128)(2,1)} async-done(((bf16[32,2,1808]{2,1,0:T(2,128)(2,1)}), bf16[32,2,1808]{2,1,0:T(2,128)(2,1)}, u32[]{:S(2)}, u32[]{:S(2)}) %all-to-all-start.3) | async-done | bytes 231456 | tf_op jit(solution)/shard_map/all_to_all | solution.py:42
  411.6 4.1 total.5
  417.8 4.1 rows_back_join.2
  436.6 5.2 %all-to-all-start.4 = ((bf16[32,2,2384]{2,1,0:T(2,128)(2,1)}), bf16[32,2,2384]{2,1,0:T(2,128)(2,1)S(1)}, u32[]{:S(2)}, u32[]{:S(2)}) async-start(bf16[32,2,2384]{2,1,0:T(2,128)(2,1)} %reshape.412), calls=%async_computation.4 | async-start | bytes 622592 | tf_op jit(solution)/shard_map/all_to_all | solution.py:42
  442.5 10.1 %collective-permute-done.51 = bf16[128,1024]{1,0:T(8,128)(2,1)} collective-permute-done((bf16[128,1024]{1,0:T(8,128)(2,1)}, bf16[128,1024]{1,0:T(8,128)(2,1)}, u32[]{:S(2)}, u32[]{:S(2)}) %collective-permute-start.51) | collective-permute-done | bytes 262176 | tf_op jit(solution)/shard_map/ppermute | solution.py:38
  454.0 3.3 rows_back_pack.3
  467.7 4.9 %rows_back_join.3 = f32[16,64,1024]{2,1,0:T(8,128)} custom-call(s32[14]{0:T(128)S(1)} %copy-done.46, bf16[10,64,1024]{2,1,0:T(8,128)(2,1)S(1)} %bitcast.160, bf16[6,64,1024]{2,1,0:T(8,128)(2,1)} %collective-permute-done.47.refs_1_, bf16[8,64,1024]{2,1,0:T(8,128)(2,1)} %collective-permute-done.48.refs_2_, bf16[16,64,1024]{2,1,0:T(8,128)(2,1)} %bitcast.189), custom_call_target="tpu_custom_call" | custom-call | flops 1024 | bytes 1024 | tf_op jit(solution)/shard_map/rows_back_join/pallas_call | solution.py:98
  (373 shorter events, 141.1 us)
Async XLA Ops:
  5.8 18.9 %collective-permute-start.1 = (bf16[32,4096]{1,0:T(8,128)(2,1)}, bf16[32,4096]{1,0:T(8,128)(2,1)S(1)}, u32[]{:S(2)}, u32[]{:S(2)}) collective-permute-start(bf16[32,4096]{1,0:T(8,128)(2,1)} %get-tuple-element.186), channel_id=1, source_target_pairs={{0,8},{4,12},{8,0},{12,4},{16,24},{20,28},{24,16},{28,20},{1,9},{5... | collective-permute-start | bytes 786440 | tf_op jit(solution)/shard_map/ppermute | solution.py:38
  5.8 18.8 %collective-permute-start.2 = (bf16[32,4096]{1,0:T(8,128)(2,1)}, bf16[32,4096]{1,0:T(8,128)(2,1)S(1)}, u32[]{:S(2)}, u32[]{:S(2)}) collective-permute-start(bf16[32,4096]{1,0:T(8,128)(2,1)} %get-tuple-element.186), channel_id=1, source_target_pairs={{0,16},{4,20},{8,24},{12,28},{16,0},{20,4},{24,8},{28,12},{1,17},{... | collective-permute-start | bytes 786440 | tf_op jit(solution)/shard_map/ppermute | solution.py:38
  8.3 25.7 %collective-permute-start.3 = (bf16[32,4096]{1,0:T(8,128)(2,1)}, bf16[32,4096]{1,0:T(8,128)(2,1)}, u32[]{:S(2)}, u32[]{:S(2)}) collective-permute-start(bf16[32,4096]{1,0:T(8,128)(2,1)} %get-tuple-element.186), channel_id=1, source_target_pairs={{0,24},{4,28},{8,16},{12,20},{16,8},{20,12},{24,0},{28,4},{1,25},{... | collective-permute-start | bytes 786440 | tf_op jit(solution)/shard_map/ppermute | solution.py:38
  13.9 32.6 %all-to-all-start = ((bf16[8,10,1024]{2,1,0:T(8,128)(2,1)}), bf16[8,10,1024]{2,1,0:T(8,128)(2,1)}, u32[]{:S(2)}, u32[]{:S(2)}) async-start(bf16[8,10,1024]{2,1,0:T(8,128)(2,1)} %broadcast_in_dim.14), calls=%async_computation | async-start | bytes 524288 | tf_op jit(solution)/shard_map/all_to_all | solution.py:1195
  35.1 22.3 %collective-permute-start.4 = (bf16[4,32,4096]{2,1,0:T(8,128)(2,1)S(1)}, bf16[4,32,4096]{2,1,0:T(8,128)(2,1)}, u32[]{:S(2)}, u32[]{:S(2)}) collective-permute-start(bf16[4,32,4096]{2,1,0:T(8,128)(2,1)S(1)} %pad_maximum_fusion.refs_0_), channel_id=1, source_target_pairs={{0,4},{4,0},{8,12},{12,8},{16,20},{20,16},{24,28},{28,24},{1,5},{5... | collective-permute-start | bytes 3145736 | tf_op jit(solution)/shard_map/ppermute | solution.py:38
  36.4 21.3 %collective-permute-start.5 = (bf16[4,32,4096]{2,1,0:T(8,128)(2,1)S(1)}, bf16[4,32,4096]{2,1,0:T(8,128)(2,1)}, u32[]{:S(2)}, u32[]{:S(2)}) collective-permute-start(bf16[4,32,4096]{2,1,0:T(8,128)(2,1)S(1)} %pad_maximum_fusion.refs_0_), channel_id=1, source_target_pairs={{0,2},{1,3},{2,0},{3,1},{4,6},{5,7},{6,4},{7,5},{8,10},{9,11},{10,... | collective-permute-start | bytes 3145736 | tf_op jit(solution)/shard_map/ppermute | solution.py:25
  47.7 18.5 %collective-permute-start.9 = (bf16[64,2048]{1,0:T(8,128)(2,1)}, bf16[64,2048]{1,0:T(8,128)(2,1)}, u32[]{:S(2)}, u32[]{:S(2)}) collective-permute-start(bf16[64,2048]{1,0:T(8,128)(2,1)} %get-tuple-element.198), channel_id=1, source_target_pairs={{0,16},{4,20},{8,24},{12,28},{16,0},{20,4},{24,8},{28,12},{1,17},{... | collective-permute-start | bytes 786440 | tf_op jit(solution)/shard_map/ppermute | solution.py:38
  66.2 32.1 %collective-permute-start.11 = (bf16[4,32,4096]{2,1,0:T(8,128)(2,1)S(1)}, bf16[4,32,4096]{2,1,0:T(8,128)(2,1)}, u32[]{:S(2)}, u32[]{:S(2)}) collective-permute-start(bf16[4,32,4096]{2,1,0:T(8,128)(2,1)S(1)} %pad_maximum_fusion.refs_0_), channel_id=1, source_target_pairs={{0,1},{1,0},{2,3},{3,2},{4,5},{5,4},{6,7},{7,6},{8,9},{9,8},{10,11... | collective-permute-start | bytes 3145736 | tf_op jit(solution)/shard_map/ppermute | solution.py:25
  68.6 29.7 %collective-permute-start.12 = (bf16[4,32,4096]{2,1,0:T(8,128)(2,1)}, bf16[4,32,4096]{2,1,0:T(8,128)(2,1)}, u32[]{:S(2)}, u32[]{:S(2)}) collective-permute-start(bf16[4,32,4096]{2,1,0:T(8,128)(2,1)} %collective-permute-done.4.refs_1_), channel_id=1, source_target_pairs={{0,1},{1,0},{2,3},{3,2},{4,5},{5,4},{6,7},{7,6},{8,9},{9,8},{10,11... | collective-permute-start | bytes 3145736 | tf_op jit(solution)/shard_map/ppermute | solution.py:25
  68.6 29.7 %collective-permute-start.13 = (bf16[4,32,4096]{2,1,0:T(8,128)(2,1)}, bf16[4,32,4096]{2,1,0:T(8,128)(2,1)}, u32[]{:S(2)}, u32[]{:S(2)}) collective-permute-start(bf16[4,32,4096]{2,1,0:T(8,128)(2,1)} %collective-permute-done.5.refs_2_), channel_id=1, source_target_pairs={{0,1},{1,0},{2,3},{3,2},{4,5},{5,4},{6,7},{7,6},{8,9},{9,8},{10,11... | collective-permute-start | bytes 3145736 | tf_op jit(solution)/shard_map/ppermute | solution.py:25
  69.1 29.2 %collective-permute-start.6 = (bf16[4,32,4096]{2,1,0:T(8,128)(2,1)}, bf16[4,32,4096]{2,1,0:T(8,128)(2,1)}, u32[]{:S(2)}, u32[]{:S(2)}) collective-permute-start(bf16[4,32,4096]{2,1,0:T(8,128)(2,1)} %collective-permute-done.5.refs_2_), channel_id=1, source_target_pairs={{0,4},{4,0},{8,12},{12,8},{16,20},{20,16},{24,28},{28,24},{1,5},{5... | collective-permute-start | bytes 3145736 | tf_op jit(solution)/shard_map/ppermute | solution.py:38
  69.4 22.3 %collective-permute-start.7 = (bf16[6,64,1024]{2,1,0:T(8,128)(2,1)}, bf16[6,64,1024]{2,1,0:T(8,128)(2,1)}, u32[]{:S(2)}, u32[]{:S(2)}) collective-permute-start(bf16[6,64,1024]{2,1,0:T(8,128)(2,1)} %get-tuple-element.185), channel_id=1, source_target_pairs={{0,2},{1,3},{2,0},{3,1},{4,6},{5,7},{6,4},{7,5},{8,10},{9,11},{10,... | collective-permute-start | bytes 2359304 | tf_op jit(solution)/shard_map/ppermute | solution.py:25
  71.6 26.8 %all-to-all-start.1 = ((f32[32,2,1536]{2,1,0:T(2,128)}), f32[32,2,1536]{2,1,0:T(2,128)S(1)}, u32[]{:S(2)}, u32[]{:S(2)}) async-start(f32[32,2,1536]{2,1,0:T(2,128)} %reshape.371), calls=%async_computation.1 | async-start | bytes 786432 | tf_op jit(solution)/shard_map/all_to_all | solution.py:42
  99.1 25.6 %collective-permute-start.15 = (bf16[8,64,1024]{2,1,0:T(8,128)(2,1)}, bf16[8,64,1024]{2,1,0:T(8,128)(2,1)S(1)}, u32[]{:S(2)}, u32[]{:S(2)}) collective-permute-start(bf16[8,64,1024]{2,1,0:T(8,128)(2,1)} %rows_send.3), channel_id=1, source_target_pairs={{0,1},{1,0},{2,3},{3,2},{4,5},{5,4},{6,7},{7,6},{8,9},{9,8},{10,11... | collective-permute-start | bytes 3145736 | tf_op jit(solution)/shard_map/ppermute | solution.py:25
  99.2 29.9 %collective-permute-start.16 = (bf16[4,64,2048]{2,1,0:T(8,128)(2,1)}, bf16[4,64,2048]{2,1,0:T(8,128)(2,1)S(1)}, u32[]{:S(2)}, u32[]{:S(2)}) collective-permute-start(bf16[4,64,2048]{2,1,0:T(8,128)(2,1)} %pad_maximum_fusion.1.refs_0_), channel_id=1, source_target_pairs={{0,4},{4,0},{8,12},{12,8},{16,20},{20,16},{24,28},{28,24},{1,5},{5... | collective-permute-start | bytes 3145736 | tf_op jit(solution)/shard_map/ppermute | solution.py:38
  99.3 30.8 %collective-permute-start.17 = (bf16[4,64,2048]{2,1,0:T(8,128)(2,1)}, bf16[4,64,2048]{2,1,0:T(8,128)(2,1)}, u32[]{:S(2)}, u32[]{:S(2)}) collective-permute-start(bf16[4,64,2048]{2,1,0:T(8,128)(2,1)} %pad_maximum_fusion.1.refs_0_), channel_id=1, source_target_pairs={{0,2},{1,3},{2,0},{3,1},{4,6},{5,7},{6,4},{7,5},{8,10},{9,11},{10,... | collective-permute-start | bytes 3145736 | tf_op jit(solution)/shard_map/ppermute | solution.py:25
  130.1 27.6 %collective-permute-start.19 = (bf16[4,64,2048]{2,1,0:T(8,128)(2,1)}, bf16[4,64,2048]{2,1,0:T(8,128)(2,1)}, u32[]{:S(2)}, u32[]{:S(2)}) collective-permute-start(bf16[4,64,2048]{2,1,0:T(8,128)(2,1)} %collective-permute-done.17.refs_2_), channel_id=1, source_target_pairs={{0,4},{4,0},{8,12},{12,8},{16,20},{20,16},{24,28},{28,24},{1,5},{5... | collective-permute-start | bytes 3145736 | tf_op jit(solution)/shard_map/ppermute | solution.py:38
  131.7 26.1 %collective-permute-start.18 = (bf16[6,64,1024]{2,1,0:T(8,128)(2,1)}, bf16[6,64,1024]{2,1,0:T(8,128)(2,1)}, u32[]{:S(2)}, u32[]{:S(2)}) collective-permute-start(bf16[6,64,1024]{2,1,0:T(8,128)(2,1)} %get-tuple-element.221), channel_id=1, source_target_pairs={{0,2},{1,3},{2,0},{3,1},{4,6},{5,7},{6,4},{7,5},{8,10},{9,11},{10,... | collective-permute-start | bytes 2359304 | tf_op jit(solution)/shard_map/ppermute | solution.py:25
  131.8 22.7 %collective-permute-start.20 = (bf16[128,1024]{1,0:T(8,128)(2,1)}, bf16[128,1024]{1,0:T(8,128)(2,1)}, u32[]{:S(2)}, u32[]{:S(2)}) collective-permute-start(bf16[128,1024]{1,0:T(8,128)(2,1)} %get-tuple-element.234), channel_id=1, source_target_pairs={{0,8},{4,12},{8,0},{12,4},{16,24},{20,28},{24,16},{28,20},{1,9},{5... | collective-permute-start | bytes 786440 | tf_op jit(solution)/shard_map/ppermute | solution.py:38
  134.3 20.2 %collective-permute-start.21 = (bf16[128,1024]{1,0:T(8,128)(2,1)}, bf16[128,1024]{1,0:T(8,128)(2,1)}, u32[]{:S(2)}, u32[]{:S(2)}) collective-permute-start(bf16[128,1024]{1,0:T(8,128)(2,1)} %get-tuple-element.234), channel_id=1, source_target_pairs={{0,16},{4,20},{8,24},{12,28},{16,0},{20,4},{24,8},{28,12},{1,17},{... | collective-permute-start | bytes 786440 | tf_op jit(solution)/shard_map/ppermute | solution.py:38
  135.3 22.5 %collective-permute-start.22 = (bf16[128,1024]{1,0:T(8,128)(2,1)}, bf16[128,1024]{1,0:T(8,128)(2,1)}, u32[]{:S(2)}, u32[]{:S(2)}) collective-permute-start(bf16[128,1024]{1,0:T(8,128)(2,1)} %get-tuple-element.234), channel_id=1, source_target_pairs={{0,24},{4,28},{8,16},{12,20},{16,8},{20,12},{24,0},{28,4},{1,25},{... | collective-permute-start | bytes 786440 | tf_op jit(solution)/shard_map/ppermute | solution.py:38
  161.9 15.5 %collective-permute-start.24 = (bf16[640,1024]{1,0:T(8,128)(2,1)}, bf16[640,1024]{1,0:T(8,128)(2,1)S(1)}, u32[]{:S(2)}, u32[]{:S(2)}) collective-permute-start(bf16[640,1024]{1,0:T(8,128)(2,1)} %gated.1.mlp_ref), channel_id=1, source_target_pairs={{0,1},{1,0},{2,3},{3,2},{4,5},{5,4},{6,7},{7,6},{8,9},{9,8},{10,11... | collective-permute-start | bytes 3932168 | tf_op jit(solution)/shard_map/ppermute | solution.py:25
  171.2 24.4 %collective-permute-start.25 = (bf16[4,128,1024]{2,1,0:T(8,128)(2,1)S(1)}, bf16[4,128,1024]{2,1,0:T(8,128)(2,1)S(1)}, u32[]{:S(2)}, u32[]{:S(2)}) collective-permute-start(bf16[4,128,1024]{2,1,0:T(8,128)(2,1)S(1)} %pad_maximum_fusion.2.refs_0_), channel_id=1, source_target_pairs={{0,4},{4,0},{8,12},{12,8},{16,20},{20,16},{24,28},{28,24},{1,5},{5... | collective-permute-start | bytes 3145736 | tf_op jit(solution)/shard_map/ppermute | solution.py:38
  171.8 24.0 %collective-permute-start.26 = (bf16[4,128,1024]{2,1,0:T(8,128)(2,1)S(1)}, bf16[4,128,1024]{2,1,0:T(8,128)(2,1)S(1)}, u32[]{:S(2)}, u32[]{:S(2)}) collective-permute-start(bf16[4,128,1024]{2,1,0:T(8,128)(2,1)S(1)} %pad_maximum_fusion.2.refs_0_), channel_id=1, source_target_pairs={{0,2},{1,3},{2,0},{3,1},{4,6},{5,7},{6,4},{7,5},{8,10},{9,11},{10,... | collective-permute-start | bytes 3145736 | tf_op jit(solution)/shard_map/ppermute | solution.py:25
  195.8 16.2 %collective-permute-start.27 = (bf16[2,128,1024]{2,1,0:T(8,128)(2,1)S(1)}, bf16[2,128,1024]{2,1,0:T(8,128)(2,1)S(1)}, u32[]{:S(2)}, u32[]{:S(2)}) collective-permute-start(bf16[2,128,1024]{2,1,0:T(8,128)(2,1)S(1)} %slice.85), channel_id=1, source_target_pairs={{0,2},{1,3},{2,0},{3,1},{4,6},{5,7},{6,4},{7,5},{8,10},{9,11},{10,... | collective-permute-start | bytes 1572872 | tf_op jit(solution)/shard_map/ppermute | solution.py:25
  197.6 35.2 %collective-permute-start.29 = (bf16[256,1024]{1,0:T(8,128)(2,1)S(1)}, bf16[256,1024]{1,0:T(8,128)(2,1)S(1)}, u32[]{:S(2)}, u32[]{:S(2)}) collective-permute-start(bf16[256,1024]{1,0:T(8,128)(2,1)S(1)} %copy-done.72), channel_id=1, source_target_pairs={{0,2},{1,3},{2,0},{3,1},{4,6},{5,7},{6,4},{7,5},{8,10},{9,11},{10,... | collective-permute-start | bytes 1572872 | tf_op jit(solution)/shard_map/ppermute | solution.py:25
  198.4 34.4 %collective-permute-start.30 = (bf16[256,1024]{1,0:T(8,128)(2,1)S(1)}, bf16[256,1024]{1,0:T(8,128)(2,1)S(1)}, u32[]{:S(2)}, u32[]{:S(2)}) collective-permute-start(bf16[256,1024]{1,0:T(8,128)(2,1)S(1)} %copy-done.71), channel_id=1, source_target_pairs={{0,4},{4,0},{8,12},{12,8},{16,20},{20,16},{24,28},{28,24},{1,5},{5... | collective-permute-start | bytes 1572872 | tf_op jit(solution)/shard_map/ppermute | solution.py:38
  234.9 22.2 %collective-permute-start.31 = (bf16[512,1024]{1,0:T(8,128)(2,1)}, bf16[512,1024]{1,0:T(8,128)(2,1)S(1)}, u32[]{:S(2)}, u32[]{:S(2)}) collective-permute-start(bf16[512,1024]{1,0:T(8,128)(2,1)} %get-tuple-element.263), channel_id=1, source_target_pairs={{0,4},{4,0},{8,12},{12,8},{16,20},{20,16},{24,28},{28,24},{1,5},{5... | collective-permute-start | bytes 3145736 | tf_op jit(solution)/shard_map/ppermute | solution.py:38
  235.9 21.9 %collective-permute-start.32 = (bf16[512,1024]{1,0:T(8,128)(2,1)}, bf16[512,1024]{1,0:T(8,128)(2,1)S(1)}, u32[]{:S(2)}, u32[]{:S(2)}) collective-permute-start(bf16[512,1024]{1,0:T(8,128)(2,1)} %get-tuple-element.264), channel_id=1, source_target_pairs={{0,2},{1,3},{2,0},{3,1},{4,6},{5,7},{6,4},{7,5},{8,10},{9,11},{10,... | collective-permute-start | bytes 3145736 | tf_op jit(solution)/shard_map/ppermute | solution.py:25
  257.8 18.6 %collective-permute-start.33 = (bf16[640,1024]{1,0:T(8,128)(2,1)}, bf16[640,1024]{1,0:T(8,128)(2,1)S(1)}, u32[]{:S(2)}, u32[]{:S(2)}) collective-permute-start(bf16[640,1024]{1,0:T(8,128)(2,1)} %get-tuple-element.269), channel_id=1, source_target_pairs={{0,1},{1,0},{2,3},{3,2},{4,5},{5,4},{6,7},{7,6},{8,9},{9,8},{10,11... | collective-permute-start | bytes 3932168 | tf_op jit(solution)/shard_map/ppermute | solution.py:25
  277.4 25.8 %collective-permute-start.36 = (bf16[640,1024]{1,0:T(8,128)(2,1)}, bf16[640,1024]{1,0:T(8,128)(2,1)}, u32[]{:S(2)}, u32[]{:S(2)}) collective-permute-start(bf16[640,1024]{1,0:T(8,128)(2,1)} %get-tuple-element.290), channel_id=1, source_target_pairs={{0,1},{1,0},{2,3},{3,2},{4,5},{5,4},{6,7},{7,6},{8,9},{9,8},{10,11... | collective-permute-start | bytes 3932168 | tf_op jit(solution)/shard_map/ppermute | solution.py:25
  278.6 51.9 %all-to-all-start.2 = ((bf16[4,128,1024]{2,1,0:T(8,128)(2,1)}), bf16[4,128,1024]{2,1,0:T(8,128)(2,1)}, u32[]{:S(2)}, u32[]{:S(2)}) async-start(bf16[4,128,1024]{2,1,0:T(8,128)(2,1)} %bitcast.200), calls=%async_computation.2 | async-start | bytes 2097152 | tf_op jit(solution)/shard_map/all_to_all | solution.py:55
  288.5 40.0 %collective-permute-start.37 = (bf16[512,1024]{1,0:T(8,128)(2,1)}, bf16[512,1024]{1,0:T(8,128)(2,1)S(1)}, u32[]{:S(2)}, u32[]{:S(2)}) collective-permute-start(bf16[512,1024]{1,0:T(8,128)(2,1)} %get-tuple-element.299), channel_id=1, source_target_pairs={{0,4},{4,0},{8,12},{12,8},{16,20},{20,16},{24,28},{28,24},{1,5},{5... | collective-permute-start | bytes 3145736 | tf_op jit(solution)/shard_map/ppermute | solution.py:38
  289.5 39.9 %collective-permute-start.38 = (bf16[512,1024]{1,0:T(8,128)(2,1)}, bf16[512,1024]{1,0:T(8,128)(2,1)S(1)}, u32[]{:S(2)}, u32[]{:S(2)}) collective-permute-start(bf16[512,1024]{1,0:T(8,128)(2,1)} %get-tuple-element.300), channel_id=1, source_target_pairs={{0,2},{1,3},{2,0},{3,1},{4,6},{5,7},{6,4},{7,5},{8,10},{9,11},{10,... | collective-permute-start | bytes 3145736 | tf_op jit(solution)/shard_map/ppermute | solution.py:25
  307.8 23.4 %collective-permute-start.39 = (bf16[6,64,1024]{2,1,0:T(8,128)(2,1)}, bf16[6,64,1024]{2,1,0:T(8,128)(2,1)}, u32[]{:S(2)}, u32[]{:S(2)}) collective-permute-start(bf16[6,64,1024]{2,1,0:T(8,128)(2,1)} %bitcast.227), channel_id=1, source_target_pairs={{0,2},{1,3},{2,0},{3,1},{4,6},{5,7},{6,4},{7,5},{8,10},{9,11},{10,... | collective-permute-start | bytes 2359304 | tf_op jit(solution)/shard_map/ppermute | solution.py:25
  348.3 27.5 %collective-permute-start.43 = (bf16[2,4,128,1024]{3,2,1,0:T(8,128)(2,1)}, bf16[2,4,128,1024]{3,2,1,0:T(8,128)(2,1)}, u32[]{:S(2)}, u32[]{:S(2)}) collective-permute-start(bf16[2,4,128,1024]{3,2,1,0:T(8,128)(2,1)} %get-tuple-element.322), channel_id=1, source_target_pairs={{0,1},{1,0},{2,3},{3,2},{4,5},{5,4},{6,7},{7,6},{8,9},{9,8},{10,11... | collective-permute-start | bytes 6291464 | tf_op jit(solution)/shard_map/ppermute | solution.py:25
  357.6 18.9 %collective-permute-start.42 = (bf16[384,1024]{1,0:T(8,128)(2,1)}, bf16[384,1024]{1,0:T(8,128)(2,1)}, u32[]{:S(2)}, u32[]{:S(2)}) collective-permute-start(bf16[384,1024]{1,0:T(8,128)(2,1)} %get-tuple-element.321), channel_id=1, source_target_pairs={{0,4},{4,0},{8,12},{12,8},{16,20},{20,16},{24,28},{28,24},{1,5},{5... | collective-permute-start | bytes 2359304 | tf_op jit(solution)/shard_map/ppermute | solution.py:38
  358.4 17.5 %collective-permute-start.41 = (bf16[128,1024]{1,0:T(8,128)(2,1)}, bf16[128,1024]{1,0:T(8,128)(2,1)S(1)}, u32[]{:S(2)}, u32[]{:S(2)}) collective-permute-start(bf16[128,1024]{1,0:T(8,128)(2,1)} %get-tuple-element.320), channel_id=1, source_target_pairs={{0,2},{1,3},{2,0},{3,1},{4,6},{5,7},{6,4},{7,5},{8,10},{9,11},{10,... | collective-permute-start | bytes 786440 | tf_op jit(solution)/shard_map/ppermute | solution.py:25
  359.3 30.8 %all-to-all-start.5 = ((bf16[4,128,1024]{2,1,0:T(8,128)(2,1)}), bf16[4,128,1024]{2,1,0:T(8,128)(2,1)}, u32[]{:S(2)}, u32[]{:S(2)}) async-start(bf16[4,128,1024]{2,1,0:T(8,128)(2,1)} %bitcast.199), calls=%async_computation.5 | async-start | bytes 2097152 | tf_op jit(solution)/shard_map/all_to_all | solution.py:55
  380.7 30.1 %collective-permute-start.44 = (bf16[512,1024]{1,0:T(8,128)(2,1)}, bf16[512,1024]{1,0:T(8,128)(2,1)}, u32[]{:S(2)}, u32[]{:S(2)}) collective-permute-start(bf16[512,1024]{1,0:T(8,128)(2,1)} %get-tuple-element.330), channel_id=1, source_target_pairs={{0,4},{4,0},{8,12},{12,8},{16,20},{20,16},{24,28},{28,24},{1,5},{5... | collective-permute-start | bytes 3145736 | tf_op jit(solution)/shard_map/ppermute | solution.py:38
  381.4 29.4 %collective-permute-start.45 = (bf16[512,1024]{1,0:T(8,128)(2,1)}, bf16[512,1024]{1,0:T(8,128)(2,1)}, u32[]{:S(2)}, u32[]{:S(2)}) collective-permute-start(bf16[512,1024]{1,0:T(8,128)(2,1)} %get-tuple-element.331), channel_id=1, source_target_pairs={{0,2},{1,3},{2,0},{3,1},{4,6},{5,7},{6,4},{7,5},{8,10},{9,11},{10,... | collective-permute-start | bytes 3145736 | tf_op jit(solution)/shard_map/ppermute | solution.py:25
  385.5 25.3 %collective-permute-start.46 = (bf16[8,64,1024]{2,1,0:T(8,128)(2,1)}, bf16[8,64,1024]{2,1,0:T(8,128)(2,1)}, u32[]{:S(2)}, u32[]{:S(2)}) collective-permute-start(bf16[8,64,1024]{2,1,0:T(8,128)(2,1)} %rows_back_pack.2), channel_id=1, source_target_pairs={{0,1},{1,0},{2,3},{3,2},{4,5},{5,4},{6,7},{7,6},{8,9},{9,8},{10,11... | collective-permute-start | bytes 3145736 | tf_op jit(solution)/shard_map/ppermute | solution.py:25
  390.2 19.2 %all-to-all-start.3 = ((bf16[32,2,1808]{2,1,0:T(2,128)(2,1)}), bf16[32,2,1808]{2,1,0:T(2,128)(2,1)}, u32[]{:S(2)}, u32[]{:S(2)}) async-start(bf16[32,2,1808]{2,1,0:T(2,128)(2,1)} %reshape.410), calls=%async_computation.3 | async-start | bytes 491520 | tf_op jit(solution)/shard_map/all_to_all | solution.py:42
  410.8 19.1 %collective-permute-start.47 = (bf16[6,64,1024]{2,1,0:T(8,128)(2,1)}, bf16[6,64,1024]{2,1,0:T(8,128)(2,1)}, u32[]{:S(2)}, u32[]{:S(2)}) collective-permute-start(bf16[6,64,1024]{2,1,0:T(8,128)(2,1)} %bitcast.226), channel_id=1, source_target_pairs={{0,2},{1,3},{2,0},{3,1},{4,6},{5,7},{6,4},{7,5},{8,10},{9,11},{10,... | collective-permute-start | bytes 2359304 | tf_op jit(solution)/shard_map/ppermute | solution.py:25
  417.8 24.0 %collective-permute-start.49 = (bf16[128,1024]{1,0:T(8,128)(2,1)}, bf16[128,1024]{1,0:T(8,128)(2,1)}, u32[]{:S(2)}, u32[]{:S(2)}) collective-permute-start(bf16[128,1024]{1,0:T(8,128)(2,1)} %get-tuple-element.379), channel_id=1, source_target_pairs={{0,8},{4,12},{8,0},{12,4},{16,24},{20,28},{24,16},{28,20},{1,9},{5... | collective-permute-start | bytes 786440 | tf_op jit(solution)/shard_map/ppermute | solution.py:38
  423.0 19.5 %collective-permute-start.50 = (bf16[128,1024]{1,0:T(8,128)(2,1)}, bf16[128,1024]{1,0:T(8,128)(2,1)}, u32[]{:S(2)}, u32[]{:S(2)}) collective-permute-start(bf16[128,1024]{1,0:T(8,128)(2,1)} %get-tuple-element.381), channel_id=1, source_target_pairs={{0,16},{4,20},{8,24},{12,28},{16,0},{20,4},{24,8},{28,12},{1,17},{... | collective-permute-start | bytes 786440 | tf_op jit(solution)/shard_map/ppermute | solution.py:38
  425.2 27.4 %collective-permute-start.51 = (bf16[128,1024]{1,0:T(8,128)(2,1)}, bf16[128,1024]{1,0:T(8,128)(2,1)}, u32[]{:S(2)}, u32[]{:S(2)}) collective-permute-start(bf16[128,1024]{1,0:T(8,128)(2,1)} %get-tuple-element.380), channel_id=1, source_target_pairs={{0,24},{4,28},{8,16},{12,20},{16,8},{20,12},{24,0},{28,4},{1,25},{... | collective-permute-start | bytes 786440 | tf_op jit(solution)/shard_map/ppermute | solution.py:38
  436.6 23.0 %all-to-all-start.4 = ((bf16[32,2,2384]{2,1,0:T(2,128)(2,1)}), bf16[32,2,2384]{2,1,0:T(2,128)(2,1)S(1)}, u32[]{:S(2)}, u32[]{:S(2)}) async-start(bf16[32,2,2384]{2,1,0:T(2,128)(2,1)} %reshape.412), calls=%async_computation.4 | async-start | bytes 622592 | tf_op jit(solution)/shard_map/all_to_all | solution.py:42
  (85 other events, 782.1 us)
where the time goes:
time: 482 us; the launch traced here: 473 us
  Pallas kernels  233 us (48%)
  starting transfers between devices  80.9 us (17%)
  waiting for transfers between devices  71.8 us (15%)
  local copies, waits for them, and re-layouts  56.7 us (12%)
  other arithmetic  16.9 us (4%)
  matrix products  10.3 us (2%)
    pallas_call x4, Pallas kernels, hidden_call(): pl.pallas_call(kernel, grid_spec=pltpu.PrefetchScalarGridSpec(num_scalar_...  61.1 us
    pallas_call x14, Pallas kernels, move_call(): pl.pallas_call(functools.partial(move_kernel, body, len(inputs) + len(out...  52.6 us
    ppermute x24, waiting for transfers between devices, swap_win(): return lax.ppermute(array, 'win', [(j, j ^ bits) for j in range(count)])  43 us
    unnamed x168, local copies, waits for them, and re-layouts  32.8 us
    ppermute x28, starting transfers between devices, swap_frm(): return lax.ppermute(array, 'frm', [(j, j ^ bit) for j in range(4)])  28.5 us
    ppermute x24, starting transfers between devices, swap_win(): return lax.ppermute(array, 'win', [(j, j ^ bits) for j in range(count)])  20.8 us
    pallas_call x1, Pallas kernels, attend_back(): pl.pallas_call(attend_back_kernel, grid=(heads // GROUP, windows), in_spe...  19.4 us
    all_to_all x3, waiting for transfers between devices, exchange_all(): return lax.all_to_all(array, BOTH, split_axis=0, concat_axis=0, tiled=True)  17.2 us
  transfers between devices with their start and end apart: 58, of which 19 were waited for; matrix products, arithmetic and copies ran while one was open for 12% of the time, Pallas kernels for 44%

commit v1 on v0

--- a/solution.py
+++ b/solution.py
@@ -384,7 +384,9 @@
 
     slots = rows.reshape(10, SPATIAL, rows.shape[1])
     shape = low_shape(8, SPATIAL, rows.shape[1])
-    return move_call(body, "rows_back_pack", where, [slots, back], [shape], 8)[0]
+    return move_call(
+        body, "rows_back_pack", where, [slots, back], [shape], 8, limit=WHOLE_LIMIT
+    )[0]
 
 
 def windows_back_join(where, rows, back, got, dead, dtype):
@@ -421,6 +423,7 @@
         [jax.ShapeDtypeStruct((16, SPATIAL, width), dtype)],
         16,
         [pltpu.VMEM((16, SPATIAL, width), bf16)],
+        WHOLE_LIMIT,
     )[0]
     return out.reshape(dead.shape)
 

time: 482 us -> 475 us (0.985)
    unnamed x168 -> x166, local copies, waits for them, and re-layouts: 32.8 us -> 28.8 us
  transfers between devices with their start and end apart: 58 -> 58, of which waited for: 19 -> 17; matrix products, arithmetic and copies ran while one was open for 12% -> 11% of each run, Pallas kernels for 44% -> 44%
where the time goes in v1:
time: 475 us; the launch traced here: 466 us
  Pallas kernels  231 us (49%)
  starting transfers between devices  80.5 us (17%)
  waiting for transfers between devices  71.2 us (15%)
  local copies, waits for them, and re-layouts  52.7 us (11%)
  other arithmetic  15.3 us (3%)
  matrix products  11.5 us (2%)
    pallas_call x4, Pallas kernels, hidden_call(): pl.pallas_call(kernel, grid_spec=pltpu.PrefetchScalarGridSpec(num_scalar_...  60.9 us
    pallas_call x14, Pallas kernels, move_call(): pl.pallas_call(functools.partial(move_kernel, body, len(inputs) + len(out...  51.8 us
    ppermute x24, waiting for transfers between devices, swap_win(): return lax.ppermute(array, 'win', [(j, j ^ bits) for j in range(count)])  41.9 us
    unnamed x166, local copies, waits for them, and re-layouts  28.8 us
    ppermute x28, starting transfers between devices, swap_frm(): return lax.ppermute(array, 'frm', [(j, j ^ bit) for j in range(4)])  28.2 us
    ppermute x24, starting transfers between devices, swap_win(): return lax.ppermute(array, 'win', [(j, j ^ bits) for j in range(count)])  20.9 us
    pallas_call x1, Pallas kernels, attend_back(): pl.pallas_call(attend_back_kernel, grid=(heads // GROUP, windows), in_spe...  19.4 us
    all_to_all x3, waiting for transfers between devices, exchange_all(): return lax.all_to_all(array, BOTH, split_axis=0, concat_axis=0, tiled=True)  17.3 us
  transfers between devices with their start and end apart: 58, of which 17 were waited for; matrix products, arithmetic and copies ran while one was open for 11% of the time, Pallas kernels for 44%

profile of v1, /device:TPU:9, one launch (start us, length us, event | category | flops | bytes accessed | tf_op | source)
XLA Modules:
  0.0 465.9 jit_solution(11626610522734175752)
XLA Ops:
  2.7 3.0 halves.1
  8.5 3.0 rows_send.2
  13.9 6.6 %all-to-all-start = ((bf16[8,10,1024]{2,1,0:T(8,128)(2,1)}), bf16[8,10,1024]{2,1,0:T(8,128)(2,1)}, u32[]{:S(2)}, u32[]{:S(2)}) async-start(bf16[8,10,1024]{2,1,0:T(8,128)(2,1)} %broadcast_in_dim.14), calls=%async_computation | async-start | bytes 524288 | tf_op jit(solution)/shard_map/all_to_all | solution.py:1198
  21.3 3.4 rows_pack.2
  24.7 9.4 %collective-permute-done.3 = bf16[32,4096]{1,0:T(8,128)(2,1)} collective-permute-done((bf16[32,4096]{1,0:T(8,128)(2,1)}, bf16[32,4096]{1,0:T(8,128)(2,1)}, u32[]{:S(2)}, u32[]{:S(2)}) %collective-permute-start.3) | collective-permute-done | bytes 262176 | tf_op jit(solution)/shard_map/ppermute | solution.py:38
  52.1 5.4 %collective-permute-done.4.refs_1_ = bf16[4,32,4096]{2,1,0:T(8,128)(2,1)} collective-permute-done((bf16[4,32,4096]{2,1,0:T(8,128)(2,1)S(1)}, bf16[4,32,4096]{2,1,0:T(8,128)(2,1)}, u32[]{:S(2)}, u32[]{:S(2)}) %collective-permute-start.4) | collective-permute-done | bytes 1048608 | tf_op jit(solution)/shard_map/ppermute | solution.py:38
  59.6 6.7 %collective-permute-done.9 = bf16[64,2048]{1,0:T(8,128)(2,1)} collective-permute-done((bf16[64,2048]{1,0:T(8,128)(2,1)}, bf16[64,2048]{1,0:T(8,128)(2,1)}, u32[]{:S(2)}, u32[]{:S(2)}) %collective-permute-start.9) | collective-permute-done | bytes 262176 | tf_op jit(solution)/shard_map/ppermute | solution.py:38
  71.6 7.0 %all-to-all-start.1 = ((f32[32,2,1536]{2,1,0:T(2,128)}), f32[32,2,1536]{2,1,0:T(2,128)S(1)}, u32[]{:S(2)}, u32[]{:S(2)}) async-start(f32[32,2,1536]{2,1,0:T(2,128)} %reshape.371), calls=%async_computation.1 | async-start | bytes 786432 | tf_op jit(solution)/shard_map/all_to_all | solution.py:42
  78.7 3.1 rows_send.3
  83.9 7.8 %collective-permute-done.7.refs_1_ = bf16[6,64,1024]{2,1,0:T(8,128)(2,1)} collective-permute-done((bf16[6,64,1024]{2,1,0:T(8,128)(2,1)}, bf16[6,64,1024]{2,1,0:T(8,128)(2,1)}, u32[]{:S(2)}, u32[]{:S(2)}) %collective-permute-start.7) | collective-permute-done | bytes 786464 | tf_op jit(solution)/shard_map/ppermute | solution.py:25
  91.7 6.6 %all-to-all-done.1 = f32[32,2,1536]{2,1,0:T(2,128)S(1)} async-done(((f32[32,2,1536]{2,1,0:T(2,128)}), f32[32,2,1536]{2,1,0:T(2,128)S(1)}, u32[]{:S(2)}, u32[]{:S(2)}) %all-to-all-start.1) | async-done | bytes 393248 | tf_op jit(solution)/shard_map/all_to_all | solution.py:42
  107.2 8.0 %place_qkv.1 = (bf16[8,2,2,32,3072]{4,3,2,1,0:T(8,128)(2,1)}, bf16[8,2,2,32,1024]{4,3,2,1,0:T(8,128)(2,1)}) custom-call(s32[14]{0:T(128)S(1)} %copy-done.44, bf16[4,32,4096]{2,1,0:T(8,128)(2,1)S(1)} %copy-done.11, bf16[4,32,4096]{2,1,0:T(8,128)(2,1)} %collective-permute-done.4.refs_1_, bf16[4,32,4096]{2,1,0:T(8,128)(2,1)} %collective-permute-done.5.refs_2_, ...), custom_call_target="tpu_custom_call" | custom-call | flops 1024 | bytes 1024 | tf_op jit(solution)/shard_map/place_qkv/pallas_call | solution.py:98
  115.3 9.6 %qkv.1 = (bf16[640,3072]{1,0:T(8,128)(2,1)}, bf16[640,1024]{1,0:T(8,128)(2,1)}) custom-call(bf16[640,1024]{1,0:T(8,128)(2,1)S(1)} %bitcast.153, f32[2,1,6144]{2,1,0:T(1,128)S(1)} %copy-done.15, bf16[1024,3072]{1,0:T(8,128)(2,1)} %bitcast.181), custom_call_target="tpu_custom_call" | custom-call | flops 1024 | bytes 1024 | tf_op jit(solution)/shard_map/qkv/pallas_call | solution.py:627
  124.8 3.4 rows_pack.3
  131.7 2.7 collective-permute-start.20
  135.6 3.1 copy.81.space_ref
  140.1 14.3 %attend.1 = (bf16[640,1024]{1,0:T(8,128)(2,1)}, bf16[2,16,320,320]{3,2,1,0:T(8,128)(2,1)}) custom-call(bf16[640,3072]{1,0:T(8,128)(2,1)} %get-tuple-element.217.q_ref.k_ref.v_ref, bf16[640,3072]{1,0:T(8,128)(2,1)} %get-tuple-element.217.q_ref.k_ref.v_ref, bf16[640,3072]{1,0:T(8,128)(2,1)} %get-tuple-element.217.q_ref.k_ref.v_ref, ...), custom_call_target="tpu_custom_call" | custom-call | flops 1024 | bytes 1024 | tf_op jit(solution)/shard_map/attend/pallas_call | solution.py:518
  154.4 3.4 collective-permute-done.22
  162.1 2.6 collective-permute-start.24
  164.7 5.2 %attn_out.1 = (bf16[640,1024]{1,0:T(8,128)(2,1)}, f32[640,1024]{1,0:T(8,128)}, bf16[640,1024]{1,0:T(8,128)(2,1)}) custom-call(bf16[640,1024]{1,0:T(8,128)(2,1)S(1)} %copy-done.7, bf16[1024,1024]{1,0:T(8,128)(2,1)} %bitcast.190, bf16[640,1024]{1,0:T(8,128)(2,1)S(1)} %bitcast.154, f32[2,1,6144]{2,1,0:T(1,128)S(1)} %copy-done.15), custom_call_target="tpu_custom_call" | custom-call | flops 1024 | bytes 1024 | tf_op jit(solution)/shard_map/attn_out/pallas_call | solution.py:655
  172.0 4.4 place_up.1
  177.5 13.0 %mlp_up.2 = (bf16[2,640,1024]{2,1,0:T(8,128)(2,1)}, bf16[2,640,1024]{2,1,0:T(8,128)(2,1)}, bf16[256,1024]{1,0:T(8,128)(2,1)}, bf16[256,1024]{1,0:T(8,128)(2,1)}, bf16[512,1024]{1,0:T(8,128)(2,1)}) custom-call(s32[14]{0:T(128)S(1)} %copy-done.44, bf16[640,1024]{1,0:T(8,128)(2,1)S(1)} %copy-done.2, bf16[640,1024]{1,0:T(8,128)(2,1)S(1)} %collective-permute-done.23.other_ref, ...), custom_call_target="tpu_custom_call" | custom-call | flops 1024 | bytes 1024 | tf_op jit(solution)/shard_map/mlp_up/pallas_call | solution.py:707
  190.5 5.4 %collective-permute-done.25.refs_1_ = bf16[4,128,1024]{2,1,0:T(8,128)(2,1)S(1)} collective-permute-done((bf16[4,128,1024]{2,1,0:T(8,128)(2,1)S(1)}, bf16[4,128,1024]{2,1,0:T(8,128)(2,1)S(1)}, u32[]{:S(2)}, u32[]{:S(2)}) %collective-permute-start.25) | collective-permute-done | bytes 1048608 | tf_op jit(solution)/shard_map/ppermute | solution.py:38
  199.1 13.1 %mlp_up.3 = (bf16[2,640,1024]{2,1,0:T(8,128)(2,1)}, bf16[2,640,1024]{2,1,0:T(8,128)(2,1)}, bf16[512,1024]{1,0:T(8,128)(2,1)}, bf16[512,1024]{1,0:T(8,128)(2,1)}) custom-call(s32[14]{0:T(128)S(1)} %copy-done.44, bf16[640,1024]{1,0:T(8,128)(2,1)S(1)} %copy-done.2, bf16[640,1024]{1,0:T(8,128)(2,1)S(1)} %collective-permute-done.23.other_ref, ...), custom_call_target="tpu_custom_call" | custom-call | flops 1024 | bytes 1024 | tf_op jit(solution)/shard_map/mlp_up/pallas_call | solution.py:707
  212.2 4.0 place_down.1
  216.2 16.7 %mlp_back.2 = (bf16[256,1024]{1,0:T(8,128)(2,1)}, bf16[256,1024]{1,0:T(8,128)(2,1)}, bf16[512,1024]{1,0:T(8,128)(2,1)}, f32[1,1024]{1,0:T(1,128)}, bf16[2,640,1024]{2,1,0:T(8,128)(2,1)}) custom-call(s32[14]{0:T(128)S(1)} %copy-done.44, bf16[640,1024]{1,0:T(8,128)(2,1)S(1)} %copy-done.2, bf16[640,1024]{1,0:T(8,128)(2,1)S(1)} %collective-permute-done.23.other_ref, ...), custom_call_target="tpu_custom_call" | custom-call | flops 1024 | bytes 1024 | tf_op jit(solution)/shard_map/mlp_back/pallas_call | solution.py:707
  236.5 18.2 %mlp_back.3 = (bf16[512,1024]{1,0:T(8,128)(2,1)}, bf16[512,1024]{1,0:T(8,128)(2,1)}, f32[1,1024]{1,0:T(1,128)}, f32[640,1024]{1,0:T(8,128)}, bf16[640,1024]{1,0:T(8,128)(2,1)}) custom-call(s32[14]{0:T(128)S(1)} %copy-done.44, bf16[640,1024]{1,0:T(8,128)(2,1)S(1)} %copy-done.2, bf16[640,1024]{1,0:T(8,128)(2,1)S(1)} %collective-permute-done.23.other_ref, ...), custom_call_target="tpu_custom_call" | custom-call | flops 1024 | bytes 1024 | tf_op jit(solution)/shard_map/mlp_back/pallas_call | solution.py:707
  254.7 2.8 collective-permute-done.31.refs_1_
  258.0 3.9 collective-permute-start.33
  262.6 9.2 %mlp_down.1 = (f32[640,1024]{1,0:T(8,128)}, bf16[640,1024]{1,0:T(8,128)(2,1)}) custom-call(bf16[2,640,1024]{2,1,0:T(8,128)(2,1)S(1)} %copy-done.14, bf16[2,640,1024]{2,1,0:T(8,128)(2,1)} %get-tuple-element.266.second_ref, bf16[2048,1024]{1,0:T(8,128)(2,1)} %bitcast.180), custom_call_target="tpu_custom_call" | custom-call | flops 1024 | bytes 1024 | tf_op jit(solution)/shard_map/mlp_down/pallas_call | solution.py:863
  278.5 4.5 all-to-all-start.2
  291.2 11.9 %mid_back.1 = (f32[640,1024]{1,0:T(8,128)}, bf16[640,1024]{1,0:T(8,128)(2,1)}, f32[2,8,1024]{2,1,0:T(8,128)}, bf16[1024,1024]{1,0:T(8,128)(2,1)}) custom-call(f32[640,1024]{1,0:T(8,128)} %get-tuple-element.268.own_ref, bf16[640,1024]{1,0:T(8,128)(2,1)S(1)} %copy-done.22, f32[640,1024]{1,0:T(8,128)} %get-tuple-element.287.mid_ref, ...), custom_call_target="tpu_custom_call" | custom-call | flops 1024 | bytes 1024 | tf_op jit(solution)/shard_map/mid_back/pallas_call | solution.py:945
  303.2 4.6 result.1
  308.1 19.4 %attend_back.1 = (bf16[3,640,1024]{2,1,0:T(8,128)(2,1)}, f32[16,64,320]{2,1,0:T(8,128)}, f32[2,16,8,320]{3,2,1,0:T(8,128)}) custom-call(bf16[640,3072]{1,0:T(8,128)(2,1)} %get-tuple-element.217.q_ref.k_ref.v_ref, bf16[640,3072]{1,0:T(8,128)(2,1)} %get-tuple-element.217.q_ref.k_ref.v_ref, bf16[640,3072]{1,0:T(8,128)(2,1)} %get-tuple-element.217.q_ref.k_ref.v_ref, ...), custom_call_target="tpu_custom_call" | custom-call | flops 1024 | bytes 1024 | tf_op jit(solution)/shard_map/attend_back/pallas_call | solution.py:537
  331.1 13.1 %qkv_grad.1 = (bf16[2,4,128,1024]{3,2,1,0:T(8,128)(2,1)S(1)}, bf16[2,4,128,1024]{3,2,1,0:T(8,128)(2,1)}, bf16[2,4,128,1024]{3,2,1,0:T(8,128)(2,1)}, bf16[2,4,128,1024]{3,2,1,0:T(8,128)(2,1)}) custom-call(s32[14]{0:T(128)S(1)} %copy-done.44, bf16[3,640,1024]{2,1,0:T(8,128)(2,1)} %get-tuple-element.317.grad_ref, bf16[640,1024]{1,0:T(8,128)(2,1)S(1)} %copy-done.19, ...), custom_call_target="tpu_custom_call" | custom-call | flops 1024 | bytes 1024 | tf_op jit(solution)/shard_map/qkv_grad/pallas_call | solution.py:1020
  353.3 3.2 first_quarters.1
  359.2 4.5 all-to-all-start.5
  365.5 10.2 %tokens_back.1 = (bf16[640,1024]{1,0:T(8,128)(2,1)}, bf16[384,1024]{1,0:T(8,128)(2,1)}, f32[2,8,1024]{2,1,0:T(8,128)}) custom-call(s32[14]{0:T(128)S(1)} %copy-done.44, bf16[3,640,1024]{2,1,0:T(8,128)(2,1)} %get-tuple-element.317.grad_ref, bf16[1024,3072]{1,0:T(8,128)(2,1)} %bitcast.182, bf16[640,1024]{1,0:T(8,128)(2,1)S(1)} %bitcast.155, ...), custom_call_target="tpu_custom_call" | custom-call | flops 1024 | bytes 1024 | tf_op jit(solution)/shard_map/tokens_back/pallas_call | solution.py:1068
  375.7 4.1 merge.5
  382.1 3.0 rows_back_pack.2
  389.7 3.8 all-to-all-start.3
  398.2 10.7 %all-to-all-done.3 = bf16[32,2,1808]{2,1,0:T(2,128)(2,1)S(1)} async-done(((bf16[32,2,1808]{2,1,0:T(2,128)(2,1)}), bf16[32,2,1808]{2,1,0:T(2,128)(2,1)S(1)}, u32[]{:S(2)}, u32[]{:S(2)}) %all-to-all-start.3) | async-done | bytes 231456 | tf_op jit(solution)/shard_map/all_to_all | solution.py:42
  410.5 3.9 total.5
  416.4 3.9 rows_back_join.2
  437.1 5.0 %all-to-all-start.4 = ((bf16[32,2,2384]{2,1,0:T(2,128)(2,1)}), bf16[32,2,2384]{2,1,0:T(2,128)(2,1)S(1)}, u32[]{:S(2)}, u32[]{:S(2)}) async-start(bf16[32,2,2384]{2,1,0:T(2,128)(2,1)} %reshape.412), calls=%async_computation.4 | async-start | bytes 622592 | tf_op jit(solution)/shard_map/all_to_all | solution.py:42
  442.1 8.8 %collective-permute-done.51 = bf16[128,1024]{1,0:T(8,128)(2,1)} collective-permute-done((bf16[128,1024]{1,0:T(8,128)(2,1)}, bf16[128,1024]{1,0:T(8,128)(2,1)}, u32[]{:S(2)}, u32[]{:S(2)}) %collective-permute-start.51) | collective-permute-done | bytes 262176 | tf_op jit(solution)/shard_map/ppermute | solution.py:38
  452.2 3.0 rows_back_pack.3
  460.7 4.7 %rows_back_join.3 = f32[16,64,1024]{2,1,0:T(8,128)} custom-call(s32[14]{0:T(128)} %concatenate.36.where.where_ref, bf16[10,64,1024]{2,1,0:T(8,128)(2,1)} %bitcast.193, bf16[6,64,1024]{2,1,0:T(8,128)(2,1)} %copy-done.46, bf16[8,64,1024]{2,1,0:T(8,128)(2,1)} %collective-permute-done.48.refs_2_, bf16[16,64,1024]{2,1,0:T(8,128)(2,1)} %bitcast.185), custom_call_target="tpu_custom_call" | custom-call | flops 1024 | bytes 1024 | tf_op jit(solution)/shard_map/rows_back_join/pallas_call | solution.py:98
  (371 shorter events, 135.7 us)
Async XLA Ops:
  5.8 18.9 %collective-permute-start.1 = (bf16[32,4096]{1,0:T(8,128)(2,1)}, bf16[32,4096]{1,0:T(8,128)(2,1)S(1)}, u32[]{:S(2)}, u32[]{:S(2)}) collective-permute-start(bf16[32,4096]{1,0:T(8,128)(2,1)} %get-tuple-element.186), channel_id=1, source_target_pairs={{0,8},{4,12},{8,0},{12,4},{16,24},{20,28},{24,16},{28,20},{1,9},{5... | collective-permute-start | bytes 786440 | tf_op jit(solution)/shard_map/ppermute | solution.py:38
  5.9 18.8 %collective-permute-start.2 = (bf16[32,4096]{1,0:T(8,128)(2,1)}, bf16[32,4096]{1,0:T(8,128)(2,1)S(1)}, u32[]{:S(2)}, u32[]{:S(2)}) collective-permute-start(bf16[32,4096]{1,0:T(8,128)(2,1)} %get-tuple-element.186), channel_id=1, source_target_pairs={{0,16},{4,20},{8,24},{12,28},{16,0},{20,4},{24,8},{28,12},{1,17},{... | collective-permute-start | bytes 786440 | tf_op jit(solution)/shard_map/ppermute | solution.py:38
  8.4 25.7 %collective-permute-start.3 = (bf16[32,4096]{1,0:T(8,128)(2,1)}, bf16[32,4096]{1,0:T(8,128)(2,1)}, u32[]{:S(2)}, u32[]{:S(2)}) collective-permute-start(bf16[32,4096]{1,0:T(8,128)(2,1)} %get-tuple-element.186), channel_id=1, source_target_pairs={{0,24},{4,28},{8,16},{12,20},{16,8},{20,12},{24,0},{28,4},{1,25},{... | collective-permute-start | bytes 786440 | tf_op jit(solution)/shard_map/ppermute | solution.py:38
  13.9 32.6 %all-to-all-start = ((bf16[8,10,1024]{2,1,0:T(8,128)(2,1)}), bf16[8,10,1024]{2,1,0:T(8,128)(2,1)}, u32[]{:S(2)}, u32[]{:S(2)}) async-start(bf16[8,10,1024]{2,1,0:T(8,128)(2,1)} %broadcast_in_dim.14), calls=%async_computation | async-start | bytes 524288 | tf_op jit(solution)/shard_map/all_to_all | solution.py:1198
  35.2 22.3 %collective-permute-start.4 = (bf16[4,32,4096]{2,1,0:T(8,128)(2,1)S(1)}, bf16[4,32,4096]{2,1,0:T(8,128)(2,1)}, u32[]{:S(2)}, u32[]{:S(2)}) collective-permute-start(bf16[4,32,4096]{2,1,0:T(8,128)(2,1)S(1)} %pad_maximum_fusion.refs_0_), channel_id=1, source_target_pairs={{0,4},{4,0},{8,12},{12,8},{16,20},{20,16},{24,28},{28,24},{1,5},{5... | collective-permute-start | bytes 3145736 | tf_op jit(solution)/shard_map/ppermute | solution.py:38
  36.5 21.3 %collective-permute-start.5 = (bf16[4,32,4096]{2,1,0:T(8,128)(2,1)S(1)}, bf16[4,32,4096]{2,1,0:T(8,128)(2,1)}, u32[]{:S(2)}, u32[]{:S(2)}) collective-permute-start(bf16[4,32,4096]{2,1,0:T(8,128)(2,1)S(1)} %pad_maximum_fusion.refs_0_), channel_id=1, source_target_pairs={{0,2},{1,3},{2,0},{3,1},{4,6},{5,7},{6,4},{7,5},{8,10},{9,11},{10,... | collective-permute-start | bytes 3145736 | tf_op jit(solution)/shard_map/ppermute | solution.py:25
  47.7 18.5 %collective-permute-start.9 = (bf16[64,2048]{1,0:T(8,128)(2,1)}, bf16[64,2048]{1,0:T(8,128)(2,1)}, u32[]{:S(2)}, u32[]{:S(2)}) collective-permute-start(bf16[64,2048]{1,0:T(8,128)(2,1)} %get-tuple-element.198), channel_id=1, source_target_pairs={{0,16},{4,20},{8,24},{12,28},{16,0},{20,4},{24,8},{28,12},{1,17},{... | collective-permute-start | bytes 786440 | tf_op jit(solution)/shard_map/ppermute | solution.py:38
  66.3 32.1 %collective-permute-start.11 = (bf16[4,32,4096]{2,1,0:T(8,128)(2,1)S(1)}, bf16[4,32,4096]{2,1,0:T(8,128)(2,1)}, u32[]{:S(2)}, u32[]{:S(2)}) collective-permute-start(bf16[4,32,4096]{2,1,0:T(8,128)(2,1)S(1)} %pad_maximum_fusion.refs_0_), channel_id=1, source_target_pairs={{0,1},{1,0},{2,3},{3,2},{4,5},{5,4},{6,7},{7,6},{8,9},{9,8},{10,11... | collective-permute-start | bytes 3145736 | tf_op jit(solution)/shard_map/ppermute | solution.py:25
  68.6 29.7 %collective-permute-start.12 = (bf16[4,32,4096]{2,1,0:T(8,128)(2,1)}, bf16[4,32,4096]{2,1,0:T(8,128)(2,1)}, u32[]{:S(2)}, u32[]{:S(2)}) collective-permute-start(bf16[4,32,4096]{2,1,0:T(8,128)(2,1)} %collective-permute-done.4.refs_1_), channel_id=1, source_target_pairs={{0,1},{1,0},{2,3},{3,2},{4,5},{5,4},{6,7},{7,6},{8,9},{9,8},{10,11... | collective-permute-start | bytes 3145736 | tf_op jit(solution)/shard_map/ppermute | solution.py:25
  68.6 29.7 %collective-permute-start.13 = (bf16[4,32,4096]{2,1,0:T(8,128)(2,1)}, bf16[4,32,4096]{2,1,0:T(8,128)(2,1)}, u32[]{:S(2)}, u32[]{:S(2)}) collective-permute-start(bf16[4,32,4096]{2,1,0:T(8,128)(2,1)} %collective-permute-done.5.refs_2_), channel_id=1, source_target_pairs={{0,1},{1,0},{2,3},{3,2},{4,5},{5,4},{6,7},{7,6},{8,9},{9,8},{10,11... | collective-permute-start | bytes 3145736 | tf_op jit(solution)/shard_map/ppermute | solution.py:25
  69.1 29.2 %collective-permute-start.6 = (bf16[4,32,4096]{2,1,0:T(8,128)(2,1)}, bf16[4,32,4096]{2,1,0:T(8,128)(2,1)}, u32[]{:S(2)}, u32[]{:S(2)}) collective-permute-start(bf16[4,32,4096]{2,1,0:T(8,128)(2,1)} %collective-permute-done.5.refs_2_), channel_id=1, source_target_pairs={{0,4},{4,0},{8,12},{12,8},{16,20},{20,16},{24,28},{28,24},{1,5},{5... | collective-permute-start | bytes 3145736 | tf_op jit(solution)/shard_map/ppermute | solution.py:38
  69.4 22.3 %collective-permute-start.7 = (bf16[6,64,1024]{2,1,0:T(8,128)(2,1)}, bf16[6,64,1024]{2,1,0:T(8,128)(2,1)}, u32[]{:S(2)}, u32[]{:S(2)}) collective-permute-start(bf16[6,64,1024]{2,1,0:T(8,128)(2,1)} %get-tuple-element.185), channel_id=1, source_target_pairs={{0,2},{1,3},{2,0},{3,1},{4,6},{5,7},{6,4},{7,5},{8,10},{9,11},{10,... | collective-permute-start | bytes 2359304 | tf_op jit(solution)/shard_map/ppermute | solution.py:25
  71.6 26.8 %all-to-all-start.1 = ((f32[32,2,1536]{2,1,0:T(2,128)}), f32[32,2,1536]{2,1,0:T(2,128)S(1)}, u32[]{:S(2)}, u32[]{:S(2)}) async-start(f32[32,2,1536]{2,1,0:T(2,128)} %reshape.371), calls=%async_computation.1 | async-start | bytes 786432 | tf_op jit(solution)/shard_map/all_to_all | solution.py:42
  99.2 25.7 %collective-permute-start.15 = (bf16[8,64,1024]{2,1,0:T(8,128)(2,1)}, bf16[8,64,1024]{2,1,0:T(8,128)(2,1)S(1)}, u32[]{:S(2)}, u32[]{:S(2)}) collective-permute-start(bf16[8,64,1024]{2,1,0:T(8,128)(2,1)} %rows_send.3), channel_id=1, source_target_pairs={{0,1},{1,0},{2,3},{3,2},{4,5},{5,4},{6,7},{7,6},{8,9},{9,8},{10,11... | collective-permute-start | bytes 3145736 | tf_op jit(solution)/shard_map/ppermute | solution.py:25
  99.2 29.9 %collective-permute-start.16 = (bf16[4,64,2048]{2,1,0:T(8,128)(2,1)}, bf16[4,64,2048]{2,1,0:T(8,128)(2,1)S(1)}, u32[]{:S(2)}, u32[]{:S(2)}) collective-permute-start(bf16[4,64,2048]{2,1,0:T(8,128)(2,1)} %pad_maximum_fusion.1.refs_0_), channel_id=1, source_target_pairs={{0,4},{4,0},{8,12},{12,8},{16,20},{20,16},{24,28},{28,24},{1,5},{5... | collective-permute-start | bytes 3145736 | tf_op jit(solution)/shard_map/ppermute | solution.py:38
  99.3 30.9 %collective-permute-start.17 = (bf16[4,64,2048]{2,1,0:T(8,128)(2,1)}, bf16[4,64,2048]{2,1,0:T(8,128)(2,1)}, u32[]{:S(2)}, u32[]{:S(2)}) collective-permute-start(bf16[4,64,2048]{2,1,0:T(8,128)(2,1)} %pad_maximum_fusion.1.refs_0_), channel_id=1, source_target_pairs={{0,2},{1,3},{2,0},{3,1},{4,6},{5,7},{6,4},{7,5},{8,10},{9,11},{10,... | collective-permute-start | bytes 3145736 | tf_op jit(solution)/shard_map/ppermute | solution.py:25
  130.2 27.6 %collective-permute-start.19 = (bf16[4,64,2048]{2,1,0:T(8,128)(2,1)}, bf16[4,64,2048]{2,1,0:T(8,128)(2,1)}, u32[]{:S(2)}, u32[]{:S(2)}) collective-permute-start(bf16[4,64,2048]{2,1,0:T(8,128)(2,1)} %collective-permute-done.17.refs_2_), channel_id=1, source_target_pairs={{0,4},{4,0},{8,12},{12,8},{16,20},{20,16},{24,28},{28,24},{1,5},{5... | collective-permute-start | bytes 3145736 | tf_op jit(solution)/shard_map/ppermute | solution.py:38
  131.7 26.1 %collective-permute-start.18 = (bf16[6,64,1024]{2,1,0:T(8,128)(2,1)}, bf16[6,64,1024]{2,1,0:T(8,128)(2,1)}, u32[]{:S(2)}, u32[]{:S(2)}) collective-permute-start(bf16[6,64,1024]{2,1,0:T(8,128)(2,1)} %get-tuple-element.221), channel_id=1, source_target_pairs={{0,2},{1,3},{2,0},{3,1},{4,6},{5,7},{6,4},{7,5},{8,10},{9,11},{10,... | collective-permute-start | bytes 2359304 | tf_op jit(solution)/shard_map/ppermute | solution.py:25
  131.7 22.7 %collective-permute-start.20 = (bf16[128,1024]{1,0:T(8,128)(2,1)}, bf16[128,1024]{1,0:T(8,128)(2,1)}, u32[]{:S(2)}, u32[]{:S(2)}) collective-permute-start(bf16[128,1024]{1,0:T(8,128)(2,1)} %get-tuple-element.234), channel_id=1, source_target_pairs={{0,8},{4,12},{8,0},{12,4},{16,24},{20,28},{24,16},{28,20},{1,9},{5... | collective-permute-start | bytes 786440 | tf_op jit(solution)/shard_map/ppermute | solution.py:38
  134.4 20.0 %collective-permute-start.21 = (bf16[128,1024]{1,0:T(8,128)(2,1)}, bf16[128,1024]{1,0:T(8,128)(2,1)}, u32[]{:S(2)}, u32[]{:S(2)}) collective-permute-start(bf16[128,1024]{1,0:T(8,128)(2,1)} %get-tuple-element.234), channel_id=1, source_target_pairs={{0,16},{4,20},{8,24},{12,28},{16,0},{20,4},{24,8},{28,12},{1,17},{... | collective-permute-start | bytes 786440 | tf_op jit(solution)/shard_map/ppermute | solution.py:38
  134.8 22.9 %collective-permute-start.22 = (bf16[128,1024]{1,0:T(8,128)(2,1)}, bf16[128,1024]{1,0:T(8,128)(2,1)}, u32[]{:S(2)}, u32[]{:S(2)}) collective-permute-start(bf16[128,1024]{1,0:T(8,128)(2,1)} %get-tuple-element.234), channel_id=1, source_target_pairs={{0,24},{4,28},{8,16},{12,20},{16,8},{20,12},{24,0},{28,4},{1,25},{... | collective-permute-start | bytes 786440 | tf_op jit(solution)/shard_map/ppermute | solution.py:38
  171.5 24.4 %collective-permute-start.25 = (bf16[4,128,1024]{2,1,0:T(8,128)(2,1)S(1)}, bf16[4,128,1024]{2,1,0:T(8,128)(2,1)S(1)}, u32[]{:S(2)}, u32[]{:S(2)}) collective-permute-start(bf16[4,128,1024]{2,1,0:T(8,128)(2,1)S(1)} %pad_maximum_fusion.2.refs_0_), channel_id=1, source_target_pairs={{0,4},{4,0},{8,12},{12,8},{16,20},{20,16},{24,28},{28,24},{1,5},{5... | collective-permute-start | bytes 3145736 | tf_op jit(solution)/shard_map/ppermute | solution.py:38
  171.6 24.4 %collective-permute-start.26 = (bf16[4,128,1024]{2,1,0:T(8,128)(2,1)S(1)}, bf16[4,128,1024]{2,1,0:T(8,128)(2,1)S(1)}, u32[]{:S(2)}, u32[]{:S(2)}) collective-permute-start(bf16[4,128,1024]{2,1,0:T(8,128)(2,1)S(1)} %pad_maximum_fusion.2.refs_0_), channel_id=1, source_target_pairs={{0,2},{1,3},{2,0},{3,1},{4,6},{5,7},{6,4},{7,5},{8,10},{9,11},{10,... | collective-permute-start | bytes 3145736 | tf_op jit(solution)/shard_map/ppermute | solution.py:25
  196.0 16.2 %collective-permute-start.27 = (bf16[2,128,1024]{2,1,0:T(8,128)(2,1)S(1)}, bf16[2,128,1024]{2,1,0:T(8,128)(2,1)S(1)}, u32[]{:S(2)}, u32[]{:S(2)}) collective-permute-start(bf16[2,128,1024]{2,1,0:T(8,128)(2,1)S(1)} %slice.85), channel_id=1, source_target_pairs={{0,2},{1,3},{2,0},{3,1},{4,6},{5,7},{6,4},{7,5},{8,10},{9,11},{10,... | collective-permute-start | bytes 1572872 | tf_op jit(solution)/shard_map/ppermute | solution.py:25
  196.4 15.8 %collective-permute-start.28 = (bf16[2,128,1024]{2,1,0:T(8,128)(2,1)S(1)}, bf16[2,128,1024]{2,1,0:T(8,128)(2,1)S(1)}, u32[]{:S(2)}, u32[]{:S(2)}) collective-permute-start(bf16[2,128,1024]{2,1,0:T(8,128)(2,1)S(1)} %slice.86), channel_id=1, source_target_pairs={{0,4},{4,0},{8,12},{12,8},{16,20},{20,16},{24,28},{28,24},{1,5},{5... | collective-permute-start | bytes 1572872 | tf_op jit(solution)/shard_map/ppermute | solution.py:38
  197.6 35.3 %collective-permute-start.29 = (bf16[256,1024]{1,0:T(8,128)(2,1)S(1)}, bf16[256,1024]{1,0:T(8,128)(2,1)S(1)}, u32[]{:S(2)}, u32[]{:S(2)}) collective-permute-start(bf16[256,1024]{1,0:T(8,128)(2,1)S(1)} %copy-done.71), channel_id=1, source_target_pairs={{0,2},{1,3},{2,0},{3,1},{4,6},{5,7},{6,4},{7,5},{8,10},{9,11},{10,... | collective-permute-start | bytes 1572872 | tf_op jit(solution)/shard_map/ppermute | solution.py:25
  198.7 34.3 %collective-permute-start.30 = (bf16[256,1024]{1,0:T(8,128)(2,1)S(1)}, bf16[256,1024]{1,0:T(8,128)(2,1)S(1)}, u32[]{:S(2)}, u32[]{:S(2)}) collective-permute-start(bf16[256,1024]{1,0:T(8,128)(2,1)S(1)} %copy-done.70), channel_id=1, source_target_pairs={{0,4},{4,0},{8,12},{12,8},{16,20},{20,16},{24,28},{28,24},{1,5},{5... | collective-permute-start | bytes 1572872 | tf_op jit(solution)/shard_map/ppermute | solution.py:38
  235.0 22.5 %collective-permute-start.31 = (bf16[512,1024]{1,0:T(8,128)(2,1)}, bf16[512,1024]{1,0:T(8,128)(2,1)S(1)}, u32[]{:S(2)}, u32[]{:S(2)}) collective-permute-start(bf16[512,1024]{1,0:T(8,128)(2,1)} %get-tuple-element.263), channel_id=1, source_target_pairs={{0,4},{4,0},{8,12},{12,8},{16,20},{20,16},{24,28},{28,24},{1,5},{5... | collective-permute-start | bytes 3145736 | tf_op jit(solution)/shard_map/ppermute | solution.py:38
  236.1 21.9 %collective-permute-start.32 = (bf16[512,1024]{1,0:T(8,128)(2,1)}, bf16[512,1024]{1,0:T(8,128)(2,1)S(1)}, u32[]{:S(2)}, u32[]{:S(2)}) collective-permute-start(bf16[512,1024]{1,0:T(8,128)(2,1)} %get-tuple-element.264), channel_id=1, source_target_pairs={{0,2},{1,3},{2,0},{3,1},{4,6},{5,7},{6,4},{7,5},{8,10},{9,11},{10,... | collective-permute-start | bytes 3145736 | tf_op jit(solution)/shard_map/ppermute | solution.py:25
  258.0 18.3 %collective-permute-start.33 = (bf16[640,1024]{1,0:T(8,128)(2,1)}, bf16[640,1024]{1,0:T(8,128)(2,1)S(1)}, u32[]{:S(2)}, u32[]{:S(2)}) collective-permute-start(bf16[640,1024]{1,0:T(8,128)(2,1)} %get-tuple-element.269), channel_id=1, source_target_pairs={{0,1},{1,0},{2,3},{3,2},{4,5},{5,4},{6,7},{7,6},{8,9},{9,8},{10,11... | collective-permute-start | bytes 3932168 | tf_op jit(solution)/shard_map/ppermute | solution.py:25
  277.3 25.8 %collective-permute-start.36 = (bf16[640,1024]{1,0:T(8,128)(2,1)}, bf16[640,1024]{1,0:T(8,128)(2,1)}, u32[]{:S(2)}, u32[]{:S(2)}) collective-permute-start(bf16[640,1024]{1,0:T(8,128)(2,1)} %get-tuple-element.290), channel_id=1, source_target_pairs={{0,1},{1,0},{2,3},{3,2},{4,5},{5,4},{6,7},{7,6},{8,9},{9,8},{10,11... | collective-permute-start | bytes 3932168 | tf_op jit(solution)/shard_map/ppermute | solution.py:25
  278.5 51.0 %all-to-all-start.2 = ((bf16[4,128,1024]{2,1,0:T(8,128)(2,1)}), bf16[4,128,1024]{2,1,0:T(8,128)(2,1)}, u32[]{:S(2)}, u32[]{:S(2)}) async-start(bf16[4,128,1024]{2,1,0:T(8,128)(2,1)} %bitcast.200), calls=%async_computation.2 | async-start | bytes 2097152 | tf_op jit(solution)/shard_map/all_to_all | solution.py:55
  288.4 39.1 %collective-permute-start.37 = (bf16[512,1024]{1,0:T(8,128)(2,1)}, bf16[512,1024]{1,0:T(8,128)(2,1)S(1)}, u32[]{:S(2)}, u32[]{:S(2)}) collective-permute-start(bf16[512,1024]{1,0:T(8,128)(2,1)} %get-tuple-element.299), channel_id=1, source_target_pairs={{0,4},{4,0},{8,12},{12,8},{16,20},{20,16},{24,28},{28,24},{1,5},{5... | collective-permute-start | bytes 3145736 | tf_op jit(solution)/shard_map/ppermute | solution.py:38
  288.7 39.8 %collective-permute-start.38 = (bf16[512,1024]{1,0:T(8,128)(2,1)}, bf16[512,1024]{1,0:T(8,128)(2,1)S(1)}, u32[]{:S(2)}, u32[]{:S(2)}) collective-permute-start(bf16[512,1024]{1,0:T(8,128)(2,1)} %get-tuple-element.300), channel_id=1, source_target_pairs={{0,2},{1,3},{2,0},{3,1},{4,6},{5,7},{6,4},{7,5},{8,10},{9,11},{10,... | collective-permute-start | bytes 3145736 | tf_op jit(solution)/shard_map/ppermute | solution.py:25
  307.8 22.0 %collective-permute-start.39 = (bf16[6,64,1024]{2,1,0:T(8,128)(2,1)}, bf16[6,64,1024]{2,1,0:T(8,128)(2,1)}, u32[]{:S(2)}, u32[]{:S(2)}) collective-permute-start(bf16[6,64,1024]{2,1,0:T(8,128)(2,1)} %bitcast.227), channel_id=1, source_target_pairs={{0,2},{1,3},{2,0},{3,1},{4,6},{5,7},{6,4},{7,5},{8,10},{9,11},{10,... | collective-permute-start | bytes 2359304 | tf_op jit(solution)/shard_map/ppermute | solution.py:25
  347.4 28.2 %collective-permute-start.43 = (bf16[2,4,128,1024]{3,2,1,0:T(8,128)(2,1)}, bf16[2,4,128,1024]{3,2,1,0:T(8,128)(2,1)}, u32[]{:S(2)}, u32[]{:S(2)}) collective-permute-start(bf16[2,4,128,1024]{3,2,1,0:T(8,128)(2,1)} %get-tuple-element.322), channel_id=1, source_target_pairs={{0,1},{1,0},{2,3},{3,2},{4,5},{5,4},{6,7},{7,6},{8,9},{9,8},{10,11... | collective-permute-start | bytes 6291464 | tf_op jit(solution)/shard_map/ppermute | solution.py:25
  356.5 19.2 %collective-permute-start.42 = (bf16[384,1024]{1,0:T(8,128)(2,1)}, bf16[384,1024]{1,0:T(8,128)(2,1)}, u32[]{:S(2)}, u32[]{:S(2)}) collective-permute-start(bf16[384,1024]{1,0:T(8,128)(2,1)} %get-tuple-element.321), channel_id=1, source_target_pairs={{0,4},{4,0},{8,12},{12,8},{16,20},{20,16},{24,28},{28,24},{1,5},{5... | collective-permute-start | bytes 2359304 | tf_op jit(solution)/shard_map/ppermute | solution.py:38
  358.0 17.7 %collective-permute-start.41 = (bf16[128,1024]{1,0:T(8,128)(2,1)}, bf16[128,1024]{1,0:T(8,128)(2,1)S(1)}, u32[]{:S(2)}, u32[]{:S(2)}) collective-permute-start(bf16[128,1024]{1,0:T(8,128)(2,1)} %get-tuple-element.320), channel_id=1, source_target_pairs={{0,2},{1,3},{2,0},{3,1},{4,6},{5,7},{6,4},{7,5},{8,10},{9,11},{10,... | collective-permute-start | bytes 786440 | tf_op jit(solution)/shard_map/ppermute | solution.py:25
  359.2 30.5 %all-to-all-start.5 = ((bf16[4,128,1024]{2,1,0:T(8,128)(2,1)}), bf16[4,128,1024]{2,1,0:T(8,128)(2,1)}, u32[]{:S(2)}, u32[]{:S(2)}) async-start(bf16[4,128,1024]{2,1,0:T(8,128)(2,1)} %bitcast.199), calls=%async_computation.5 | async-start | bytes 2097152 | tf_op jit(solution)/shard_map/all_to_all | solution.py:55
  379.8 29.6 %collective-permute-start.44 = (bf16[512,1024]{1,0:T(8,128)(2,1)}, bf16[512,1024]{1,0:T(8,128)(2,1)S(1)}, u32[]{:S(2)}, u32[]{:S(2)}) collective-permute-start(bf16[512,1024]{1,0:T(8,128)(2,1)} %get-tuple-element.330), channel_id=1, source_target_pairs={{0,4},{4,0},{8,12},{12,8},{16,20},{20,16},{24,28},{28,24},{1,5},{5... | collective-permute-start | bytes 3145736 | tf_op jit(solution)/shard_map/ppermute | solution.py:38
  381.0 28.4 %collective-permute-start.45 = (bf16[512,1024]{1,0:T(8,128)(2,1)}, bf16[512,1024]{1,0:T(8,128)(2,1)}, u32[]{:S(2)}, u32[]{:S(2)}) collective-permute-start(bf16[512,1024]{1,0:T(8,128)(2,1)} %get-tuple-element.331), channel_id=1, source_target_pairs={{0,2},{1,3},{2,0},{3,1},{4,6},{5,7},{6,4},{7,5},{8,10},{9,11},{10,... | collective-permute-start | bytes 3145736 | tf_op jit(solution)/shard_map/ppermute | solution.py:25
  385.1 24.3 %collective-permute-start.46 = (bf16[8,64,1024]{2,1,0:T(8,128)(2,1)}, bf16[8,64,1024]{2,1,0:T(8,128)(2,1)}, u32[]{:S(2)}, u32[]{:S(2)}) collective-permute-start(bf16[8,64,1024]{2,1,0:T(8,128)(2,1)} %rows_back_pack.2), channel_id=1, source_target_pairs={{0,1},{1,0},{2,3},{3,2},{4,5},{5,4},{6,7},{7,6},{8,9},{9,8},{10,11... | collective-permute-start | bytes 3145736 | tf_op jit(solution)/shard_map/ppermute | solution.py:25
  389.7 19.2 %all-to-all-start.3 = ((bf16[32,2,1808]{2,1,0:T(2,128)(2,1)}), bf16[32,2,1808]{2,1,0:T(2,128)(2,1)S(1)}, u32[]{:S(2)}, u32[]{:S(2)}) async-start(bf16[32,2,1808]{2,1,0:T(2,128)(2,1)} %reshape.410), calls=%async_computation.3 | async-start | bytes 491520 | tf_op jit(solution)/shard_map/all_to_all | solution.py:42
  409.4 19.1 %collective-permute-start.47 = (bf16[6,64,1024]{2,1,0:T(8,128)(2,1)}, bf16[6,64,1024]{2,1,0:T(8,128)(2,1)S(1)}, u32[]{:S(2)}, u32[]{:S(2)}) collective-permute-start(bf16[6,64,1024]{2,1,0:T(8,128)(2,1)} %bitcast.226), channel_id=1, source_target_pairs={{0,2},{1,3},{2,0},{3,1},{4,6},{5,7},{6,4},{7,5},{8,10},{9,11},{10,... | collective-permute-start | bytes 2359304 | tf_op jit(solution)/shard_map/ppermute | solution.py:25
  416.4 25.7 %collective-permute-start.49 = (bf16[128,1024]{1,0:T(8,128)(2,1)}, bf16[128,1024]{1,0:T(8,128)(2,1)}, u32[]{:S(2)}, u32[]{:S(2)}) collective-permute-start(bf16[128,1024]{1,0:T(8,128)(2,1)} %get-tuple-element.379), channel_id=1, source_target_pairs={{0,8},{4,12},{8,0},{12,4},{16,24},{20,28},{24,16},{28,20},{1,9},{5... | collective-permute-start | bytes 786440 | tf_op jit(solution)/shard_map/ppermute | solution.py:38
  421.4 20.7 %collective-permute-start.50 = (bf16[128,1024]{1,0:T(8,128)(2,1)}, bf16[128,1024]{1,0:T(8,128)(2,1)}, u32[]{:S(2)}, u32[]{:S(2)}) collective-permute-start(bf16[128,1024]{1,0:T(8,128)(2,1)} %get-tuple-element.381), channel_id=1, source_target_pairs={{0,16},{4,20},{8,24},{12,28},{16,0},{20,4},{24,8},{28,12},{1,17},{... | collective-permute-start | bytes 786440 | tf_op jit(solution)/shard_map/ppermute | solution.py:38
  423.5 27.3 %collective-permute-start.51 = (bf16[128,1024]{1,0:T(8,128)(2,1)}, bf16[128,1024]{1,0:T(8,128)(2,1)}, u32[]{:S(2)}, u32[]{:S(2)}) collective-permute-start(bf16[128,1024]{1,0:T(8,128)(2,1)} %get-tuple-element.380), channel_id=1, source_target_pairs={{0,24},{4,28},{8,16},{12,20},{16,8},{20,12},{24,0},{28,4},{1,25},{... | collective-permute-start | bytes 786440 | tf_op jit(solution)/shard_map/ppermute | solution.py:38
  437.1 20.9 %all-to-all-start.4 = ((bf16[32,2,2384]{2,1,0:T(2,128)(2,1)}), bf16[32,2,2384]{2,1,0:T(2,128)(2,1)S(1)}, u32[]{:S(2)}, u32[]{:S(2)}) async-start(bf16[32,2,2384]{2,1,0:T(2,128)(2,1)} %reshape.412), calls=%async_computation.4 | async-start | bytes 622592 | tf_op jit(solution)/shard_map/all_to_all | solution.py:42
  (84 other events, 760.0 us)
